TPU v7x, 256 devices: a whole 4x4x8 slice. The times are simulated.
256 devices in a mesh: heads: 8 (over x, core), seq: 32 (over y, z).
Axes of the slice: x: 4, y: 4, z: 8, core: 2. Of those that a mesh axis runs over, the one named last changes fastest.
Arguments:
- tokens: bfloat16 [8192, 4096], P('seq'), may hold values from -6 to 6
- norm_gain: float32 [4096], replicated, may hold values from 0.1 to 1.9
- w_query: bfloat16 [4096, 4096], P(None, 'heads'), may hold values from -0.09375 to 0.09375
- w_key: bfloat16 [4096, 1024], P(None, 'heads'), may hold values from -0.1875 to 0.1875
- w_value: bfloat16 [4096, 1024], P(None, 'heads'), may hold values from -0.375 to 0.375
- w_out: bfloat16 [4096, 4096], P('heads'), may hold values from -0.09375 to 0.09375
- cache_keys: bfloat16 [8, 32768, 128], P('heads', 'seq'), may hold values from -360 to 360
- cache_values: bfloat16 [8, 32768, 128], P('heads', 'seq'), may hold values from -24 to 24
- vert_blocks: int32 [8, 64], P('heads'), may hold values from -1 to 511, as said below
- vert_count: int32 [8], P('heads'), may hold values from 32 to 64
- slash_offsets: int32 [8, 4], P('heads'), may hold values from -1 to 4, as said below
- slash_count: int32 [8], P('heads'), may hold values from 1 to 4
Outputs:
- layer_out: bfloat16 [8192, 4096], P('seq', 'heads')
Inputs may be any that keep to these rules, and one draw needn't show every extreme that they name: `vert_blocks`: row g lists cache blocks for key/value head g: its entries before vert_count[g] are distinct, the rest are -1. The cache of one index of seq holds at most 8 of the blocks that a row lists, and exactly 8 for one index in every row. `slash_offsets`: entries of row g before slash_count[g] are distinct, the rest are -1.
All inputs are finite; a program needn't handle non-finite values.
Results may differ from a plain program's by a relative error of at most 0.015.
The roundings to bfloat16 on the way count: a program that leaves them out, or rounds other values in their place, can miss the bound.
Values may be sent and summed in bfloat16 or wider, within the bound.
No kernel may reach another device: no remote copies, remote signals or barrier semaphores. Data moves between devices by JAX's collectives and lax.ppermute only.
A program may use at most 64 MiB of HBM per device.

v0:
```python
import functools
import math

import jax
import jax.numpy as jnp
from jax import lax
from jax.experimental import pallas as pl
from jax.experimental.pallas import tpu as pltpu
from jax.sharding import PartitionSpec as P

BLK = 64
HD = 128
GROUP = 4
NY = 4
NZ = 8
NX = 4
HALF = 4
VMEM = pltpu.VMEM
VSPEC = pl.BlockSpec(memory_space=pltpu.VMEM)
HSPEC = pl.BlockSpec(memory_space=pltpu.HBM)
SSPEC = pl.BlockSpec(memory_space=pltpu.SMEM)
SCALE2 = math.log2(math.e) / math.sqrt(HD)
NEG = -jnp.inf


def params(mib):
    return pltpu.CompilerParams(vmem_limit_bytes=mib << 20)


def cost(us):
    return pl.CostEstimate(flops=int(us * 1e9), bytes_accessed=0, transcendentals=0)


def tie(*values):
    return lax.optimization_barrier(values)


def shift_y(block, d):
    return lax.ppermute(
        block, "seq", [(y * NZ + z, (y + d) % NY * NZ + z) for y in range(NY) for z in range(NZ)]
    )


def shift_z(block, d):
    return lax.ppermute(
        block, "seq", [(y * NZ + z, y * NZ + (z + d) % NZ) for y in range(NY) for z in range(NZ)]
    )


def shift_x(block, d):
    return lax.ppermute(
        block, "heads", [(2 * x + c, 2 * ((x + d) % NX) + c) for x in range(NX) for c in range(2)]
    )


def swap_core(block):
    return lax.ppermute(block, "heads", [(i, i ^ 1) for i in range(2 * NX)])


def position():
    me = lax.axis_index("seq")
    return me // NZ, lax.rem(me, NZ)


def at(tab, group):
    return tab[64 + group]


def pick_kernel(tab, ck, cv, *refs):
    outs, sems = refs[:NY], refs[NY]
    y, z = position()
    group = z * NY + y
    start = at(tab, group)
    size = at(tab, group + 1) - start
    copies = []
    for dy in range(NY):
        for j in range(2):
            i = ((y + dy - start) & 3) + 4 * j
            entry = tab[jnp.minimum(start + i, 63)]
            row = pl.multiple_of(jnp.where(i < size, entry & 15, 0) * BLK, BLK)
            for k, cache in enumerate((ck, cv)):
                copies.append(
                    pltpu.make_async_copy(
                        cache.at[0, pl.ds(row, BLK)], outs[dy].at[j, k], sems.at[len(copies)]
                    )
                )
    for copy in copies:
        copy.start()
    for copy in copies:
        copy.wait()


def column_kernel(tab, r0, r1, r2, r3, *outs):
    y, z = position()
    recv = (r0, r1, r2, r3)
    start = at(tab, z * NY)
    size = at(tab, z * NY + NY) - start
    first = (y - start) & 3
    for part, out in enumerate(outs):

        def fill(i, carry):
            off = first + 4 * (HALF * part + i)
            live = off < size
            r = jnp.minimum(start + off, 63)
            hy = (tab[r] >> 4) & 3
            j = jnp.where(live, (r - at(tab, z * NY + hy)) >> 2, 0)
            d = jnp.where(live, (y - hy) & 3, 0)
            for k in range(NY):

                @pl.when(d == k)
                def _():
                    out[i] = recv[k][j]

            return carry

        lax.fori_loop(0, HALF, fill, 0)


def row_kernel(tab, *refs):
    y, z = position()
    recv, outs = refs[:-2], refs[-2:]
    for part, out in enumerate(outs):

        def fill(m, carry):
            r = y + 4 * (8 * part + m)
            live = r < at(tab, 32)
            zs = jnp.where(live, tab[r] >> 6, z)
            start = at(tab, zs * NY)
            first = (y - start) & 3
            i = jnp.where(live, (r - start - first) >> 2, 0)
            source = ((z - zs) & 7) + NZ * (i >> 2)
            slot = i & 3
            place = pl.multiple_of(m * BLK, BLK)
            for k in range(len(recv)):

                @pl.when(source == k)
                def _():
                    out[0, pl.ds(place, BLK), :] = recv[k][slot, 0]
                    out[1, pl.ds(place, BLK), :] = recv[k][slot, 1]

            return carry

        lax.fori_loop(0, 8, fill, 0)


def near_kernel(offs, cnt, q, kp, vp, k, v, m_out, l_out, acc_out):
    me = lax.axis_index("seq")
    rows = k.shape[0]
    keys = jnp.concatenate([kp[...], k[...]], axis=0)
    values = jnp.concatenate([vp[...], v[...]], axis=0)
    t = lax.broadcasted_iota(jnp.int32, (rows, 2 * rows), 0)
    u = lax.broadcasted_iota(jnp.int32, (rows, 2 * rows), 1) - rows
    gap = (t >> 6) - (u >> 6)
    hit = (gap == 0) & (u <= t)
    for e in range(4):
        off = jnp.where((e < cnt[0]) & (offs[0, e] >= 0), offs[0, e], -100)
        hit = hit | (gap == off)
    hit = hit & (u >= jnp.where(me > 0, -rows, 0))
    for h in range(GROUP):
        s = lax.dot_general(
            q[:, h * HD : (h + 1) * HD],
            keys,
            (((1,), (1,)), ((), ())),
            preferred_element_type=jnp.float32,
        )
        s = jnp.where(hit, s, NEG)
        top = jnp.broadcast_to(jnp.max(s, axis=1, keepdims=True), (rows, HD))
        p = jnp.exp2((s - across(top, 2 * rows)) * SCALE2)
        m_out[h] = top
        l_out[h] = lane_sums(p)
        acc_out[h] = jnp.dot(p.astype(jnp.bfloat16), values, preferred_element_type=jnp.float32)


def across(x, width):
    return jnp.concatenate([x] * (width // HD), axis=1)


def lane_sums(p):
    total = p[:, :HD]
    for i in range(HD, p.shape[1], HD):
        total = total + p[:, i : i + HD]
    return total


def scores_of(q, h, k):
    return lax.dot_general(
        q[:, h * HD : (h + 1) * HD], k, (((1,), (1,)), ((), ())), preferred_element_type=jnp.float32
    )


def across(x, width):
    return jnp.concatenate([x] * (width // HD), axis=1)


def lane_sums(p):
    total = p[:, :HD]
    for i in range(HD, p.shape[1], HD):
        total = total + p[:, i : i + HD]
    return total


def scores_of(q, h, k):
    return lax.dot_general(
        q[:, h * HD : (h + 1) * HD], k, (((1,), (1,)), ((), ())), preferred_element_type=jnp.float32
    )


def update(scores, values, live, old, total, acc):
    masked, base = [], 0
    for s in scores:
        key = base + lax.broadcasted_iota(jnp.int32, s.shape, 1)
        masked.append(jnp.where(key < live, s, NEG))
        base += s.shape[1]
    top = functools.reduce(jnp.maximum, [jnp.max(s, axis=1, keepdims=True) for s in masked])
    top = jnp.maximum(old, jnp.broadcast_to(top, old.shape))
    factor = jnp.exp2((old - top) * SCALE2)
    total, acc = total * factor, acc * factor
    for s, v in zip(masked, values):
        p = jnp.exp2((s - across(top, s.shape[1])) * SCALE2)
        total = total + lane_sums(p)
        acc = acc + jnp.dot(p.astype(jnp.bfloat16), v, preferred_element_type=jnp.float32)
    return top, total, acc


def row_sum(total):
    return jnp.broadcast_to(jnp.sum(total, axis=1, keepdims=True), total.shape)


def each_head(tab, shift, q, lo, hi, m_in, l_in, acc_in):
    y, _ = position()
    live = ((at(tab, 32) - ((y - shift) & 3) + 3) >> 2) * BLK
    following = [scores_of(q, 0, lo[0]), scores_of(q, 0, hi[0])]
    for h in range(GROUP):
        current = following
        if h + 1 < GROUP:
            following = [scores_of(q, h + 1, lo[0]), scores_of(q, h + 1, hi[0])]
        yield h, update(current, (lo[1], hi[1]), live, m_in[h], l_in[h], acc_in[h])


def far_kernel(shift, tab, q, lo, hi, m_in, l_in, acc_in, m_out, l_out, acc_out):
    for h, new in each_head(tab, shift, q, lo, hi, m_in, l_in, acc_in):
        m_out[h], l_out[h], acc_out[h] = new


def last_kernel(shift, tab, q, lo, hi, m_in, l_in, acc_in, att):
    for h, (_, total, acc) in each_head(tab, shift, q, lo, hi, m_in, l_in, acc_in):
        att[:, h * HD : (h + 1) * HD] = (acc / row_sum(total)).astype(jnp.bfloat16)


def product_kernel(cols, att, w, out):
    out[0] = jnp.dot(att[...], w[...], preferred_element_type=jnp.float32).astype(out.dtype)


def halves_kernel(mine, recv, a, b):
    total = (mine[2] + recv[2].astype(jnp.float32)).astype(a.dtype)
    half = a.shape[0]
    a[...] = total[:half]
    b[...] = total[half:]


def pass_kernel(mine, recv, a, b, right, left):
    half = a.shape[0]
    forth = mine[1] + recv[1].astype(jnp.float32)
    back = mine[3] + recv[3].astype(jnp.float32)
    right[:half] = (forth[:half] + a[...].astype(jnp.float32)).astype(right.dtype)
    right[half:] = forth[half:].astype(right.dtype)
    left[:half] = back[:half].astype(left.dtype)
    left[half:] = (back[half:] + b[...].astype(jnp.float32)).astype(left.dtype)


def final_kernel(mine, recv, a, b, out):
    total = mine[0] + recv[0].astype(jnp.float32)
    total = total + a[...].astype(jnp.float32) + b[...].astype(jnp.float32)
    out[...] = total.astype(out.dtype)


def local(
    tokens,
    norm_gain,
    w_query,
    w_key,
    w_value,
    w_out,
    cache_keys,
    cache_values,
    vert_blocks,
    vert_count,
    slash_offsets,
    slash_count,
):
    rows = tokens.shape[0]
    bf16 = jnp.bfloat16
    f32 = jnp.float32
    blocks = vert_blocks[0]
    index = jnp.arange(128, dtype=jnp.int32)
    entry = index[:64]
    key = jnp.where(
        entry < vert_count[0],
        (((blocks >> 4) & 7) << 6) | ((blocks >> 7) << 4) | (blocks & 15),
        4096 + entry,
    )
    edges = jnp.concatenate([key, entry * 16])
    below = jnp.sum((key[None, :] < edges[:, None]).astype(jnp.int32), axis=1)
    ranked = jnp.sum(jnp.where(below[None, :64] == index[:, None], key[None, :], 0), axis=1)
    tab = jnp.where(index < 64, ranked, below)
    heads = lax.axis_index("heads")
    x, core = heads // 2, lax.rem(heads, 2)
    order = ((x + entry[:NX]) & 3) * 2
    column_ends = below[64 : 64 + 4 * NZ + 1 : 4]
    crowded = jnp.any(column_ends[1:] - column_ends[:-1] > 4 * HALF)
    tab, away_cols, home_cols, crowded = tie(tab, order + 1 - core, order + core, crowded)

    slot = jax.ShapeDtypeStruct((2, 2, BLK, HD), bf16)
    picked = pl.pallas_call(
        pick_kernel,
        out_shape=[slot] * NY,
        in_specs=[SSPEC, HSPEC, HSPEC],
        out_specs=[VSPEC] * NY,
        scratch_shapes=[pltpu.SemaphoreType.DMA((16,))],
        compiler_params=params(60),
        cost_estimate=cost(0.7),
        name="pick",
    )(tab, cache_keys, cache_values)
    spread = [picked[0]] + [shift_y(picked[d], d) for d in range(1, NY)]
    activation = tokens.astype(f32)
    normed = (
        activation
        * lax.rsqrt(jnp.mean(activation * activation, axis=-1, keepdims=True) + 1e-05)
        * norm_gain
    ).astype(bf16)
    spread[3], normed = tie(spread[3], normed)
    quarter = jax.ShapeDtypeStruct((HALF, 2, BLK, HD), bf16)
    column, rest = pl.pallas_call(
        column_kernel,
        out_shape=[quarter] * 2,
        in_specs=[SSPEC] + [VSPEC] * NY,
        out_specs=[VSPEC] * 2,
        compiler_params=params(8),
        cost_estimate=cost(0.8),
        name="column",
    )(tab, *spread)
    key_rows = jnp.dot(normed, w_key, preferred_element_type=f32).astype(bf16)
    value_rows = jnp.dot(normed, w_value, preferred_element_type=f32).astype(bf16)
    queries = jnp.dot(normed, w_query, preferred_element_type=f32).astype(bf16)
    seqs = lax.axis_size("seq")
    route = [(i, (i + 1) % seqs) for i in range(seqs)]

    def along_z(block, between=lambda *phase: phase):
        ring = [block] + [None] * 7
        first = [shift_z(block, d) for d in (2, -2, 1, -1)]
        ring[2], ring[6], ring[1], ring[7] = between(*first)
        ring[3], ring[5] = shift_z(ring[2], 1), shift_z(ring[6], -1)
        ring[4] = shift_z(ring[2], 2)
        return ring

    made = []

    def between(*phase):
        *phase, keys, values, rows_made = tie(*phase, key_rows, value_rows, queries)
        made.extend((keys, values, rows_made))
        return phase

    ring = along_z(column, between)
    key_rows, value_rows, queries = made
    before_keys, before_values = lax.ppermute((key_rows, value_rows), "seq", route)
    half = jax.ShapeDtypeStruct((2, 8 * BLK, HD), bf16)

    def compact(*sources):
        return tuple(
            pl.pallas_call(
                row_kernel,
                out_shape=[half] * 2,
                in_specs=[SSPEC] + [VSPEC] * len(sources),
                out_specs=[VSPEC] * 2,
                compiler_params=params(16),
                cost_estimate=cost(1.3),
                name="row",
            )(tab, *sources)
        )

    rest, before_keys, before_values = tie(rest, before_keys, before_values)
    own = lax.cond(
        crowded,
        lambda rest, *ring: compact(*ring, *along_z(rest)),
        lambda rest, *ring: compact(*ring),
        rest,
        *ring,
    )
    own_lo, own_hi, near_queries = tie(*own, queries)
    own = (own_lo, own_hi)
    state_shape = [jax.ShapeDtypeStruct((GROUP, rows, HD), f32)] * 3
    state = pl.pallas_call(
        near_kernel,
        out_shape=state_shape,
        in_specs=[SSPEC] * 2 + [VSPEC] * 5,
        out_specs=[VSPEC] * 3,
        compiler_params=params(16),
        cost_estimate=cost(2.2),
        name="near",
    )(slash_offsets, slash_count, near_queries, before_keys, before_values, key_rows, value_rows)

    def far(shift, part, state):
        return pl.pallas_call(
            functools.partial(far_kernel, shift),
            out_shape=state_shape,
            in_specs=[SSPEC] + [VSPEC] * 6,
            out_specs=[VSPEC] * 3,
            compiler_params=params(16),
            cost_estimate=cost(1.8),
            name="far",
        )(tab, queries, *part, *state)

    lo1, hi3 = shift_y(own[0], 1), shift_y(own[1], -1)
    hi1, lo3 = shift_y(own[1], 1), shift_y(own[0], -1)
    state = far(0, own, state)
    lo2, hi2 = shift_y(lo1, 1), shift_y(hi3, -1)
    state = far(1, (lo1, hi1), state)
    state = far(3, (lo3, hi3), state)
    attended = pl.pallas_call(
        functools.partial(last_kernel, 2),
        out_shape=jax.ShapeDtypeStruct((rows, GROUP * HD), bf16),
        in_specs=[SSPEC] + [VSPEC] * 6,
        out_specs=VSPEC,
        compiler_params=params(16),
        cost_estimate=cost(2.5),
        name="last",
    )(tab, queries, lo2, hi2, *state)

    depth = GROUP * HD

    def product(cols, dtype):
        return pl.pallas_call(
            product_kernel,
            out_shape=jax.ShapeDtypeStruct((NX, rows, depth), dtype),
            grid_spec=pltpu.PrefetchScalarGridSpec(
                num_scalar_prefetch=1,
                grid=(NX,),
                in_specs=[
                    pl.BlockSpec((rows, depth), lambda i, cols: (0, 0)),
                    pl.BlockSpec((depth, depth), lambda i, cols: (0, cols[i])),
                ],
                out_specs=pl.BlockSpec((1, rows, depth), lambda i, cols: (i, 0, 0)),
            ),
            compiler_params=params(16),
            cost_estimate=cost(2),
            name="product",
        )(cols, attended, w_out)

    def small(kernel, count, shape, name, *operands):
        return pl.pallas_call(
            kernel,
            out_shape=[jax.ShapeDtypeStruct(shape, bf16)] * count,
            in_specs=[VSPEC] * len(operands),
            out_specs=[VSPEC] * count,
            compiler_params=params(16),
            cost_estimate=cost(0.4),
            name=name,
        )(*operands)

    away = product(away_cols, bf16)
    recv = swap_core(away)
    mine = product(home_cols, f32)
    upper, lower = small(halves_kernel, 2, (rows // 2, depth), "halves", mine, recv)
    upper, lower = shift_x(upper, 1), shift_x(lower, -1)
    right, left = small(pass_kernel, 2, (rows, depth), "pass", mine, recv, upper, lower)
    right, left = shift_x(right, 1), shift_x(left, -1)
    return small(final_kernel, 1, (rows, depth), "final", mine, recv, right, left)[0]


def solution(mesh):
    return jax.shard_map(
        local,
        mesh=mesh,
        in_specs=(
            P("seq", None),
            P(),
            P(None, "heads"),
            P(None, "heads"),
            P(None, "heads"),
            P("heads", None),
            P("heads", "seq", None),
            P("heads", "seq", None),
            P("heads", None),
            P("heads"),
            P("heads", None),
            P("heads"),
        ),
        out_specs=P("seq", "heads"),
        check_vma=False,
    )
```

profile of v0, /device:TPU:6, one launch (start us, length us, event | category | flops | bytes accessed | tf_op | source)
XLA Modules:
  0.0 92.6 jit_solution(4612019810987543324)
XLA Ops:
  0.8 0.7 compare_select_fusion
  1.9 0.8 compare_reduce_fusion
  2.7 2.4 %pick.1 = (bf16[2,2,64,128]{3,2,1,0:T(8,128)(2,1)}, bf16[2,2,64,128]{3,2,1,0:T(8,128)(2,1)}, bf16[2,2,64,128]{3,2,1,0:T(8,128)(2,1)}, bf16[2,2,64,128]{3,2,1,0:T(8,128)(2,1)}) custom-call(s32[128]{0:T(128)S(1)} %compare_select_fusion.1.tab, bf16[1,1024,128]{2,1,0:T(8,128)(2,1)} %ck.1, bf16[1,1024,128]{2,1,0:T(8,128)(2,1)} %cv.1), custom_call_target="tpu_custom_call" | custom-call | flops 700000000 | tf_op jit(solution)/shard_map/pick/pallas_call | solution.py:314
  5.1 3.1 %collective-permute-start.9 = (bf16[2,2,64,128]{3,2,1,0:T(8,128)(2,1)}, bf16[2,2,64,128]{3,2,1,0:T(8,128)(2,1)S(1)}, u32[]{:S(2)}, u32[]{:S(2)}) collective-permute-start(bf16[2,2,64,128]{3,2,1,0:T(8,128)(2,1)} %get-tuple-element.110), channel_id=1, source_target_pairs={{0,24},{1,25},{2,26},{3,27},{4,28},{5,29},{6,30},{7,31},{8,0},{9,1... | collective-permute-start | bytes 196616 | tf_op jit(solution)/shard_map/ppermute | solution.py:39
  8.2 2.2 %collective-permute-start.8 = (bf16[2,2,64,128]{3,2,1,0:T(8,128)(2,1)}, bf16[2,2,64,128]{3,2,1,0:T(8,128)(2,1)S(1)}, u32[]{:S(2)}, u32[]{:S(2)}) collective-permute-start(bf16[2,2,64,128]{3,2,1,0:T(8,128)(2,1)} %get-tuple-element.109), channel_id=1, source_target_pairs={{0,16},{1,17},{2,18},{3,19},{4,20},{5,21},{6,22},{7,23},{8,24},{9,... | collective-permute-start | bytes 196616 | tf_op jit(solution)/shard_map/ppermute | solution.py:39
  10.9 0.6 fusion.2
  11.6 3.1 %collective-permute-done.7.r1 = bf16[2,2,64,128]{3,2,1,0:T(8,128)(2,1)S(1)} collective-permute-done((bf16[2,2,64,128]{3,2,1,0:T(8,128)(2,1)}, bf16[2,2,64,128]{3,2,1,0:T(8,128)(2,1)S(1)}, u32[]{:S(2)}, u32[]{:S(2)}) %collective-permute-start.7) | collective-permute-done | bytes 65568 | tf_op jit(solution)/shard_map/ppermute | solution.py:39
  14.7 0.9 column.1
  15.6 3.3 %collective-permute-start.10 = (bf16[4,2,64,128]{3,2,1,0:T(8,128)(2,1)S(1)}, bf16[4,2,64,128]{3,2,1,0:T(8,128)(2,1)S(1)}, u32[]{:S(2)}, u32[]{:S(2)}) collective-permute-start(bf16[4,2,64,128]{3,2,1,0:T(8,128)(2,1)S(1)} %get-tuple-element.112), channel_id=1, source_target_pairs={{0,2},{1,3},{2,4},{3,5},{4,6},{5,7},{6,0},{7,1},{8,10},{9,11},{10,... | collective-permute-start | bytes 393224 | tf_op jit(solution)/shard_map/ppermute | solution.py:45
  18.9 3.1 %collective-permute-start.11 = (bf16[4,2,64,128]{3,2,1,0:T(8,128)(2,1)S(1)}, bf16[4,2,64,128]{3,2,1,0:T(8,128)(2,1)S(1)}, u32[]{:S(2)}, u32[]{:S(2)}) collective-permute-start(bf16[4,2,64,128]{3,2,1,0:T(8,128)(2,1)S(1)} %get-tuple-element.112), channel_id=1, source_target_pairs={{0,6},{1,7},{2,0},{3,1},{4,2},{5,3},{6,4},{7,5},{8,14},{9,15},{10,... | collective-permute-start | bytes 393224 | tf_op jit(solution)/shard_map/ppermute | solution.py:45
  22.0 1.0 %collective-permute-start.12 = (bf16[4,2,64,128]{3,2,1,0:T(8,128)(2,1)S(1)}, bf16[4,2,64,128]{3,2,1,0:T(8,128)(2,1)S(1)}, u32[]{:S(2)}, u32[]{:S(2)}) collective-permute-start(bf16[4,2,64,128]{3,2,1,0:T(8,128)(2,1)S(1)} %get-tuple-element.112), channel_id=1, source_target_pairs={{0,1},{1,2},{2,3},{3,4},{4,5},{5,6},{6,7},{7,0},{8,9},{9,10},{10,1... | collective-permute-start | bytes 393224 | tf_op jit(solution)/shard_map/ppermute | solution.py:45
  23.0 2.2 %collective-permute-start.13 = (bf16[4,2,64,128]{3,2,1,0:T(8,128)(2,1)S(1)}, bf16[4,2,64,128]{3,2,1,0:T(8,128)(2,1)S(1)}, u32[]{:S(2)}, u32[]{:S(2)}) collective-permute-start(bf16[4,2,64,128]{3,2,1,0:T(8,128)(2,1)S(1)} %get-tuple-element.112), channel_id=1, source_target_pairs={{0,7},{1,0},{2,1},{3,2},{4,3},{5,4},{6,5},{7,6},{8,15},{9,8},{10,9... | collective-permute-start | bytes 393224 | tf_op jit(solution)/shard_map/ppermute | solution.py:45
  25.3 1.2 %convolution_convert_fusion.q = bf16[256,512]{1,0:T(8,128)(2,1)S(1)} fusion(bf16[256,4096]{1,0:T(8,128)(2,1)S(1)} %fusion.2, bf16[4096,512]{1,0:T(8,128)(2,1)S(1)} %copy-done.7), kind=kOutput, calls=%fused_computation.5 | convolution fusion | flops 1073872896 | bytes 6553600 | tf_op jit(solution)/shard_map/dot_general | solution.py:344
  26.6 0.7 convolution_convert_fusion.1.v
  27.3 0.5 copy-done.5
  27.8 0.7 convolution_convert_fusion.2.k
  28.5 0.6 collective-permute-done.11
  29.2 1.3 %collective-permute-done.13 = bf16[4,2,64,128]{3,2,1,0:T(8,128)(2,1)S(1)} collective-permute-done((bf16[4,2,64,128]{3,2,1,0:T(8,128)(2,1)S(1)}, bf16[4,2,64,128]{3,2,1,0:T(8,128)(2,1)S(1)}, u32[]{:S(2)}, u32[]{:S(2)}) %collective-permute-start.13) | collective-permute-done | bytes 131104 | tf_op jit(solution)/shard_map/ppermute | solution.py:45
  30.5 1.0 %collective-permute-start.14 = (bf16[4,2,64,128]{3,2,1,0:T(8,128)(2,1)S(1)}, bf16[4,2,64,128]{3,2,1,0:T(8,128)(2,1)S(1)}, u32[]{:S(2)}, u32[]{:S(2)}) collective-permute-start(bf16[4,2,64,128]{3,2,1,0:T(8,128)(2,1)S(1)} %collective-permute-done.10), channel_id=1, source_target_pairs={{0,1},{1,2},{2,3},{3,4},{4,5},{5,6},{6,7},{7,0},{8,9},{9,10},{10,1... | collective-permute-start | bytes 393224 | tf_op jit(solution)/shard_map/ppermute | solution.py:45
  31.5 3.9 %collective-permute-start.15 = (bf16[4,2,64,128]{3,2,1,0:T(8,128)(2,1)S(1)}, bf16[4,2,64,128]{3,2,1,0:T(8,128)(2,1)S(1)}, u32[]{:S(2)}, u32[]{:S(2)}) collective-permute-start(bf16[4,2,64,128]{3,2,1,0:T(8,128)(2,1)S(1)} %collective-permute-done.10), channel_id=1, source_target_pairs={{0,2},{1,3},{2,4},{3,5},{4,6},{5,7},{6,0},{7,1},{8,10},{9,11},{10,... | collective-permute-start | bytes 393224 | tf_op jit(solution)/shard_map/ppermute | solution.py:45
  35.4 1.3 %collective-permute-start.16 = (bf16[4,2,64,128]{3,2,1,0:T(8,128)(2,1)S(1)}, bf16[4,2,64,128]{3,2,1,0:T(8,128)(2,1)S(1)}, u32[]{:S(2)}, u32[]{:S(2)}) collective-permute-start(bf16[4,2,64,128]{3,2,1,0:T(8,128)(2,1)S(1)} %collective-permute-done.11), channel_id=1, source_target_pairs={{0,7},{1,0},{2,1},{3,2},{4,3},{5,4},{6,5},{7,6},{8,15},{9,8},{10,9... | collective-permute-start | bytes 393224 | tf_op jit(solution)/shard_map/ppermute | solution.py:45
  36.7 0.7 collective-permute-start.17
  37.4 0.5 collective-permute-start.18
  39.2 6.4 %collective-permute-done.17.kp = bf16[256,128]{1,0:T(8,128)(2,1)S(1)} collective-permute-done((bf16[256,128]{1,0:T(8,128)(2,1)S(1)}, bf16[256,128]{1,0:T(8,128)(2,1)S(1)}, u32[]{:S(2)}, u32[]{:S(2)}) %collective-permute-start.17) | collective-permute-done | bytes 65568 | tf_op jit(solution)/shard_map/ppermute | solution.py:365
  45.6 0.7 collective-permute-done.18.vp
  46.4 1.6 %conditional.1 = ((bf16[2,512,128]{2,1,0:T(8,128)(2,1)S(1)}, bf16[2,512,128]{2,1,0:T(8,128)(2,1)S(1)})) conditional(s32[]{:T(128)} %convert_element_type.27, (s32[128]{0:T(128)S(1)}, bf16[4,2,64,128]{3,2,1,0:T(8,128)(2,1)S(1)}, bf16[4,2,64,128]{3,2,1,0:T(8,128)(2,1)S(1)}, bf16[4,2,64,128]{3,2,1,0:T(8,128)(2,1)S(1)}, ...), branch_computations={%region_4.5_spmd, %region_5.6_spmd} | conditional | flops 1300000000 | bytes 3670304 | solution.py:382
  46.4 1.6 %row.2 = (bf16[2,512,128]{2,1,0:T(8,128)(2,1)S(1)}, bf16[2,512,128]{2,1,0:T(8,128)(2,1)S(1)}) custom-call(s32[128]{0:T(128)S(1)} %get-tuple-element.43.tab, bf16[4,2,64,128]{3,2,1,0:T(8,128)(2,1)S(1)} %get-tuple-element.44.refs_0_, bf16[4,2,64,128]{3,2,1,0:T(8,128)(2,1)S(1)} %get-tuple-element.45.refs_1_, ...), custom_call_target="tpu_custom_call" | custom-call | flops 1300000000 | tf_op jit(solution)/shard_map/cond/branch_0_fun/row/pallas_call | solution.py:370
  48.1 3.1 %collective-permute-start.21 = (bf16[2,512,128]{2,1,0:T(8,128)(2,1)S(1)}, bf16[2,512,128]{2,1,0:T(8,128)(2,1)S(1)}, u32[]{:S(2)}, u32[]{:S(2)}) collective-permute-start(bf16[2,512,128]{2,1,0:T(8,128)(2,1)S(1)} %get-tuple-element.127.hi), channel_id=1, source_target_pairs={{0,24},{1,25},{2,26},{3,27},{4,28},{5,29},{6,30},{7,31},{8,0},{9,1... | collective-permute-start | bytes 786440 | tf_op jit(solution)/shard_map/ppermute | solution.py:39
  51.3 3.2 %collective-permute-start.23 = (bf16[2,512,128]{2,1,0:T(8,128)(2,1)S(1)}, bf16[2,512,128]{2,1,0:T(8,128)(2,1)S(1)}, u32[]{:S(2)}, u32[]{:S(2)}) collective-permute-start(bf16[2,512,128]{2,1,0:T(8,128)(2,1)S(1)} %get-tuple-element.126.lo), channel_id=1, source_target_pairs={{0,24},{1,25},{2,26},{3,27},{4,28},{5,29},{6,30},{7,31},{8,0},{9,1... | collective-permute-start | bytes 786440 | tf_op jit(solution)/shard_map/ppermute | solution.py:39
  54.5 2.2 %near.1 = (f32[4,256,128]{2,1,0:T(8,128)S(1)}, f32[4,256,128]{2,1,0:T(8,128)S(1)}, f32[4,256,128]{2,1,0:T(8,128)S(1)}) custom-call(s32[1,4]{1,0:T(1,128)S(1)} %copy-done.2, s32[1]{0:T(128)S(6)} %copy.18.cnt, bf16[256,512]{1,0:T(8,128)(2,1)S(1)} %convolution_convert_fusion.q, bf16[256,128]{1,0:T(8,128)(2,1)S(1)} %collective-permute-done.17.kp, ...), custom_call_target="tpu_custom_call" | custom-call | flops 2200000000 | tf_op jit(solution)/shard_map/near/pallas_call | solution.py:392
  56.7 2.2 %far.3 = (f32[4,256,128]{2,1,0:T(8,128)S(1)}, f32[4,256,128]{2,1,0:T(8,128)S(1)}, f32[4,256,128]{2,1,0:T(8,128)S(1)}) custom-call(s32[128]{0:T(128)S(1)} %compare_select_fusion.1.tab, bf16[256,512]{1,0:T(8,128)(2,1)S(1)} %convolution_convert_fusion.q, bf16[2,512,128]{2,1,0:T(8,128)(2,1)S(1)} %get-tuple-element.126.lo, ...), custom_call_target="tpu_custom_call" | custom-call | flops 1800000000 | tf_op jit(solution)/shard_map/far/pallas_call | solution.py:403
  58.9 2.3 %collective-permute-done.19.lo = bf16[2,512,128]{2,1,0:T(8,128)(2,1)S(1)} collective-permute-done((bf16[2,512,128]{2,1,0:T(8,128)(2,1)S(1)}, bf16[2,512,128]{2,1,0:T(8,128)(2,1)S(1)}, u32[]{:S(2)}, u32[]{:S(2)}) %collective-permute-start.19) | collective-permute-done | bytes 262176 | tf_op jit(solution)/shard_map/ppermute | solution.py:39
  61.2 3.2 %collective-permute-start.22 = (bf16[2,512,128]{2,1,0:T(8,128)(2,1)S(1)}, bf16[2,512,128]{2,1,0:T(8,128)(2,1)S(1)}, u32[]{:S(2)}, u32[]{:S(2)}) collective-permute-start(bf16[2,512,128]{2,1,0:T(8,128)(2,1)S(1)} %collective-permute-done.21.hi), channel_id=1, source_target_pairs={{0,24},{1,25},{2,26},{3,27},{4,28},{5,29},{6,30},{7,31},{8,0},{9,1... | collective-permute-start | bytes 786440 | tf_op jit(solution)/shard_map/ppermute | solution.py:39
  64.4 2.1 %far.4 = (f32[4,256,128]{2,1,0:T(8,128)S(1)}, f32[4,256,128]{2,1,0:T(8,128)S(1)}, f32[4,256,128]{2,1,0:T(8,128)S(1)}) custom-call(s32[128]{0:T(128)S(1)} %compare_select_fusion.1.tab, bf16[256,512]{1,0:T(8,128)(2,1)S(1)} %convolution_convert_fusion.q, bf16[2,512,128]{2,1,0:T(8,128)(2,1)S(1)} %collective-permute-done.19.lo, ...), custom_call_target="tpu_custom_call" | custom-call | flops 1800000000 | tf_op jit(solution)/shard_map/far/pallas_call | solution.py:403
  66.6 2.1 %far.5 = (f32[4,256,128]{2,1,0:T(8,128)S(1)}, f32[4,256,128]{2,1,0:T(8,128)S(1)}, f32[4,256,128]{2,1,0:T(8,128)S(1)}) custom-call(s32[128]{0:T(128)S(1)} %compare_select_fusion.1.tab, bf16[256,512]{1,0:T(8,128)(2,1)S(1)} %convolution_convert_fusion.q, bf16[2,512,128]{2,1,0:T(8,128)(2,1)S(1)} %collective-permute-done.23.lo, ...), custom_call_target="tpu_custom_call" | custom-call | flops 1800000000 | tf_op jit(solution)/shard_map/far/pallas_call | solution.py:403
  68.8 2.2 %last.1.att = bf16[256,512]{1,0:T(8,128)(2,1)S(1)} custom-call(s32[128]{0:T(128)S(1)} %compare_select_fusion.1.tab, bf16[256,512]{1,0:T(8,128)(2,1)S(1)} %convolution_convert_fusion.q, bf16[2,512,128]{2,1,0:T(8,128)(2,1)S(1)} %collective-permute-done.20.lo, bf16[2,512,128]{2,1,0:T(8,128)(2,1)S(1)} %collective-permute-done.22.hi, ...), custom_call_target="tpu_custom_call" | custom-call | flops 2500000000 | tf_op jit(solution)/shard_map/last/pallas_call | solution.py:419
  71.0 2.0 %product.3 = bf16[4,256,512]{2,1,0:T(8,128)(2,1)S(1)} custom-call(s32[4]{0:T(128)S(1)} %get-tuple-element.143.cols, bf16[256,512]{1,0:T(8,128)(2,1)S(1)} %last.1.att, bf16[512,4096]{1,0:T(8,128)(2,1)S(1)} %copy-done.1), custom_call_target="tpu_custom_call" | custom-call | flops 2000000000 | tf_op jit(solution)/shard_map/product/pallas_call | solution.py:432
  73.1 2.0 %product.2.mine = f32[4,256,512]{2,1,0:T(8,128)S(1)} custom-call(s32[4]{0:T(128)S(1)} %get-tuple-element.105.cols, bf16[256,512]{1,0:T(8,128)(2,1)S(1)} %last.1.att, bf16[512,4096]{1,0:T(8,128)(2,1)S(1)} %copy-done.1), custom_call_target="tpu_custom_call" | custom-call | flops 2000000000 | tf_op jit(solution)/shard_map/product/pallas_call | solution.py:432
  75.0 0.7 collective-permute-done.25.recv
  75.8 0.6 collective-permute-start.26
  76.3 1.5 %collective-permute-start.27 = (bf16[128,512]{1,0:T(8,128)(2,1)S(1)}, bf16[128,512]{1,0:T(8,128)(2,1)S(1)}, u32[]{:S(2)}, u32[]{:S(2)}) collective-permute-start(bf16[128,512]{1,0:T(8,128)(2,1)S(1)} %get-tuple-element.145), channel_id=1, source_target_pairs={{0,192},{32,224},{64,0},{96,32},{128,64},{160,96},{192,128},{224,1... | collective-permute-start | bytes 393224 | tf_op jit(solution)/shard_map/ppermute | solution.py:51
  77.9 3.5 %collective-permute-done.26.a = bf16[128,512]{1,0:T(8,128)(2,1)S(1)} collective-permute-done((bf16[128,512]{1,0:T(8,128)(2,1)S(1)}, bf16[128,512]{1,0:T(8,128)(2,1)S(1)}, u32[]{:S(2)}, u32[]{:S(2)}) %collective-permute-start.26) | collective-permute-done | bytes 131104 | tf_op jit(solution)/shard_map/ppermute | solution.py:51
  81.4 1.4 %collective-permute-done.27.b = bf16[128,512]{1,0:T(8,128)(2,1)S(1)} collective-permute-done((bf16[128,512]{1,0:T(8,128)(2,1)S(1)}, bf16[128,512]{1,0:T(8,128)(2,1)S(1)}, u32[]{:S(2)}, u32[]{:S(2)}) %collective-permute-start.27) | collective-permute-done | bytes 131104 | tf_op jit(solution)/shard_map/ppermute | solution.py:51
  82.9 0.5 collective-permute-start.28
  83.5 1.6 %collective-permute-start.29 = (bf16[256,512]{1,0:T(8,128)(2,1)S(1)}, bf16[256,512]{1,0:T(8,128)(2,1)S(1)}, u32[]{:S(2)}, u32[]{:S(2)}) collective-permute-start(bf16[256,512]{1,0:T(8,128)(2,1)S(1)} %get-tuple-element.147), channel_id=1, source_target_pairs={{0,192},{32,224},{64,0},{96,32},{128,64},{160,96},{192,128},{224,1... | collective-permute-start | bytes 786440 | tf_op jit(solution)/shard_map/ppermute | solution.py:51
  85.0 5.2 %collective-permute-done.28.a = bf16[256,512]{1,0:T(8,128)(2,1)S(1)} collective-permute-done((bf16[256,512]{1,0:T(8,128)(2,1)S(1)}, bf16[256,512]{1,0:T(8,128)(2,1)S(1)}, u32[]{:S(2)}, u32[]{:S(2)}) %collective-permute-start.28) | collective-permute-done | bytes 262176 | tf_op jit(solution)/shard_map/ppermute | solution.py:51
  90.2 1.5 %collective-permute-done.29.b = bf16[256,512]{1,0:T(8,128)(2,1)S(1)} collective-permute-done((bf16[256,512]{1,0:T(8,128)(2,1)S(1)}, bf16[256,512]{1,0:T(8,128)(2,1)S(1)}, u32[]{:S(2)}, u32[]{:S(2)}) %collective-permute-start.29) | collective-permute-done | bytes 262176 | tf_op jit(solution)/shard_map/ppermute | solution.py:51
  91.8 0.8 final.1
  (44 shorter events, 1.7 us)
Async XLA Ops:
  0.0 26.5 %copy-start = (bf16[4096,128]{1,0:T(8,128)(2,1)S(1)}, bf16[4096,128]{1,0:T(8,128)(2,1)}, u32[]{:S(2)}) copy-start(bf16[4096,128]{1,0:T(8,128)(2,1)} %param.18) | copy-start | bytes 3145732
  0.0 10.4 %copy-start.4 = (bf16[256,4096]{1,0:T(8,128)(2,1)S(1)}, bf16[256,4096]{1,0:T(8,128)(2,1)}, u32[]{:S(2)}) copy-start(bf16[256,4096]{1,0:T(8,128)(2,1)} %param.14) | copy-start | bytes 6291460
  2.7 8.2 %copy-start.6 = (f32[4096]{0:T(1024)S(1)}, f32[4096]{0:T(1024)}, u32[]{:S(2)}) copy-start(f32[4096]{0:T(1024)} %param.15) | copy-start | bytes 49156
  5.1 6.5 %collective-permute-start.9 = (bf16[2,2,64,128]{3,2,1,0:T(8,128)(2,1)}, bf16[2,2,64,128]{3,2,1,0:T(8,128)(2,1)S(1)}, u32[]{:S(2)}, u32[]{:S(2)}) collective-permute-start(bf16[2,2,64,128]{3,2,1,0:T(8,128)(2,1)} %get-tuple-element.110), channel_id=1, source_target_pairs={{0,24},{1,25},{2,26},{3,27},{4,28},{5,29},{6,30},{7,31},{8,0},{9,1... | collective-permute-start | bytes 196616 | tf_op jit(solution)/shard_map/ppermute | solution.py:39
  8.2 6.5 %collective-permute-start.7 = (bf16[2,2,64,128]{3,2,1,0:T(8,128)(2,1)}, bf16[2,2,64,128]{3,2,1,0:T(8,128)(2,1)S(1)}, u32[]{:S(2)}, u32[]{:S(2)}) collective-permute-start(bf16[2,2,64,128]{3,2,1,0:T(8,128)(2,1)} %get-tuple-element.108), channel_id=1, source_target_pairs={{0,8},{1,9},{2,10},{3,11},{4,12},{5,13},{6,14},{7,15},{8,16},{9,17... | collective-permute-start | bytes 196616 | tf_op jit(solution)/shard_map/ppermute | solution.py:39
  8.2 6.5 %collective-permute-start.8 = (bf16[2,2,64,128]{3,2,1,0:T(8,128)(2,1)}, bf16[2,2,64,128]{3,2,1,0:T(8,128)(2,1)S(1)}, u32[]{:S(2)}, u32[]{:S(2)}) collective-permute-start(bf16[2,2,64,128]{3,2,1,0:T(8,128)(2,1)} %get-tuple-element.109), channel_id=1, source_target_pairs={{0,16},{1,17},{2,18},{3,19},{4,20},{5,21},{6,22},{7,23},{8,24},{9,... | collective-permute-start | bytes 196616 | tf_op jit(solution)/shard_map/ppermute | solution.py:39
  10.9 3.8 %copy-start.3 = (bf16[2,2,64,128]{3,2,1,0:T(8,128)(2,1)S(1)}, bf16[2,2,64,128]{3,2,1,0:T(8,128)(2,1)}, u32[]{:S(2)}) copy-start(bf16[2,2,64,128]{3,2,1,0:T(8,128)(2,1)} %get-tuple-element.107.r0) | copy-start | bytes 196612
  10.9 14.4 %copy-start.7 = (bf16[4096,512]{1,0:T(8,128)(2,1)S(1)}, bf16[4096,512]{1,0:T(8,128)(2,1)}, u32[]{:S(2)}) copy-start(bf16[4096,512]{1,0:T(8,128)(2,1)} %param.16) | copy-start | bytes 12582916
  15.6 12.9 %collective-permute-start.10 = (bf16[4,2,64,128]{3,2,1,0:T(8,128)(2,1)S(1)}, bf16[4,2,64,128]{3,2,1,0:T(8,128)(2,1)S(1)}, u32[]{:S(2)}, u32[]{:S(2)}) collective-permute-start(bf16[4,2,64,128]{3,2,1,0:T(8,128)(2,1)S(1)} %get-tuple-element.112), channel_id=1, source_target_pairs={{0,2},{1,3},{2,4},{3,5},{4,6},{5,7},{6,0},{7,1},{8,10},{9,11},{10,... | collective-permute-start | bytes 393224 | tf_op jit(solution)/shard_map/ppermute | solution.py:45
  18.9 10.2 %collective-permute-start.11 = (bf16[4,2,64,128]{3,2,1,0:T(8,128)(2,1)S(1)}, bf16[4,2,64,128]{3,2,1,0:T(8,128)(2,1)S(1)}, u32[]{:S(2)}, u32[]{:S(2)}) collective-permute-start(bf16[4,2,64,128]{3,2,1,0:T(8,128)(2,1)S(1)} %get-tuple-element.112), channel_id=1, source_target_pairs={{0,6},{1,7},{2,0},{3,1},{4,2},{5,3},{6,4},{7,5},{8,14},{9,15},{10,... | collective-permute-start | bytes 393224 | tf_op jit(solution)/shard_map/ppermute | solution.py:45
  22.0 7.2 %collective-permute-start.12 = (bf16[4,2,64,128]{3,2,1,0:T(8,128)(2,1)S(1)}, bf16[4,2,64,128]{3,2,1,0:T(8,128)(2,1)S(1)}, u32[]{:S(2)}, u32[]{:S(2)}) collective-permute-start(bf16[4,2,64,128]{3,2,1,0:T(8,128)(2,1)S(1)} %get-tuple-element.112), channel_id=1, source_target_pairs={{0,1},{1,2},{2,3},{3,4},{4,5},{5,6},{6,7},{7,0},{8,9},{9,10},{10,1... | collective-permute-start | bytes 393224 | tf_op jit(solution)/shard_map/ppermute | solution.py:45
  23.0 7.5 %collective-permute-start.13 = (bf16[4,2,64,128]{3,2,1,0:T(8,128)(2,1)S(1)}, bf16[4,2,64,128]{3,2,1,0:T(8,128)(2,1)S(1)}, u32[]{:S(2)}, u32[]{:S(2)}) collective-permute-start(bf16[4,2,64,128]{3,2,1,0:T(8,128)(2,1)S(1)} %get-tuple-element.112), channel_id=1, source_target_pairs={{0,7},{1,0},{2,1},{3,2},{4,3},{5,4},{6,5},{7,6},{8,15},{9,8},{10,9... | collective-permute-start | bytes 393224 | tf_op jit(solution)/shard_map/ppermute | solution.py:45
  26.5 1.2 %copy-start.5 = (bf16[4096,128]{1,0:T(8,128)(2,1)S(1)}, bf16[4096,128]{1,0:T(8,128)(2,1)}, u32[]{:S(2)}) copy-start(bf16[4096,128]{1,0:T(8,128)(2,1)} %param.17) | copy-start | bytes 3145732
  30.5 15.8 %collective-permute-start.14 = (bf16[4,2,64,128]{3,2,1,0:T(8,128)(2,1)S(1)}, bf16[4,2,64,128]{3,2,1,0:T(8,128)(2,1)S(1)}, u32[]{:S(2)}, u32[]{:S(2)}) collective-permute-start(bf16[4,2,64,128]{3,2,1,0:T(8,128)(2,1)S(1)} %collective-permute-done.10), channel_id=1, source_target_pairs={{0,1},{1,2},{2,3},{3,4},{4,5},{5,6},{6,7},{7,0},{8,9},{9,10},{10,1... | collective-permute-start | bytes 393224 | tf_op jit(solution)/shard_map/ppermute | solution.py:45
  31.5 14.8 %collective-permute-start.15 = (bf16[4,2,64,128]{3,2,1,0:T(8,128)(2,1)S(1)}, bf16[4,2,64,128]{3,2,1,0:T(8,128)(2,1)S(1)}, u32[]{:S(2)}, u32[]{:S(2)}) collective-permute-start(bf16[4,2,64,128]{3,2,1,0:T(8,128)(2,1)S(1)} %collective-permute-done.10), channel_id=1, source_target_pairs={{0,2},{1,3},{2,4},{3,5},{4,6},{5,7},{6,0},{7,1},{8,10},{9,11},{10,... | collective-permute-start | bytes 393224 | tf_op jit(solution)/shard_map/ppermute | solution.py:45
  35.4 11.0 %collective-permute-start.16 = (bf16[4,2,64,128]{3,2,1,0:T(8,128)(2,1)S(1)}, bf16[4,2,64,128]{3,2,1,0:T(8,128)(2,1)S(1)}, u32[]{:S(2)}, u32[]{:S(2)}) collective-permute-start(bf16[4,2,64,128]{3,2,1,0:T(8,128)(2,1)S(1)} %collective-permute-done.11), channel_id=1, source_target_pairs={{0,7},{1,0},{2,1},{3,2},{4,3},{5,4},{6,5},{7,6},{8,15},{9,8},{10,9... | collective-permute-start | bytes 393224 | tf_op jit(solution)/shard_map/ppermute | solution.py:45
  36.7 9.0 %collective-permute-start.17 = (bf16[256,128]{1,0:T(8,128)(2,1)S(1)}, bf16[256,128]{1,0:T(8,128)(2,1)S(1)}, u32[]{:S(2)}, u32[]{:S(2)}) collective-permute-start(bf16[256,128]{1,0:T(8,128)(2,1)S(1)} %convolution_convert_fusion.2.k), channel_id=1, source_target_pairs={{0,1},{1,2},{2,3},{3,4},{4,5},{5,6},{6,7},{7,8},{8,9},{9,10},{10,1... | collective-permute-start | bytes 196616 | tf_op jit(solution)/shard_map/ppermute | solution.py:365
  37.4 8.9 %collective-permute-start.18 = (bf16[256,128]{1,0:T(8,128)(2,1)S(1)}, bf16[256,128]{1,0:T(8,128)(2,1)S(1)}, u32[]{:S(2)}, u32[]{:S(2)}) collective-permute-start(bf16[256,128]{1,0:T(8,128)(2,1)S(1)} %convolution_convert_fusion.1.v), channel_id=1, source_target_pairs={{0,1},{1,2},{2,3},{3,4},{4,5},{5,6},{6,7},{7,8},{8,9},{9,10},{10,1... | collective-permute-start | bytes 196616 | tf_op jit(solution)/shard_map/ppermute | solution.py:365
  46.3 8.2 %copy-start.2 = (s32[1,4]{1,0:T(1,128)S(1)}, s32[1,4]{1,0:T(1,128)}, u32[]{:S(2)}) copy-start(s32[1,4]{1,0:T(1,128)} %offs.1) | copy-start | bytes 52
  47.9 16.5 %collective-permute-start.24 = (bf16[2,512,128]{2,1,0:T(8,128)(2,1)S(1)}, bf16[2,512,128]{2,1,0:T(8,128)(2,1)S(1)}, u32[]{:S(2)}, u32[]{:S(2)}) collective-permute-start(bf16[2,512,128]{2,1,0:T(8,128)(2,1)S(1)} %get-tuple-element.127.hi), channel_id=1, source_target_pairs={{0,8},{1,9},{2,10},{3,11},{4,12},{5,13},{6,14},{7,15},{8,16},{9,17... | collective-permute-start | bytes 786440 | tf_op jit(solution)/shard_map/ppermute | solution.py:39
  48.1 13.0 %collective-permute-start.21 = (bf16[2,512,128]{2,1,0:T(8,128)(2,1)S(1)}, bf16[2,512,128]{2,1,0:T(8,128)(2,1)S(1)}, u32[]{:S(2)}, u32[]{:S(2)}) collective-permute-start(bf16[2,512,128]{2,1,0:T(8,128)(2,1)S(1)} %get-tuple-element.127.hi), channel_id=1, source_target_pairs={{0,24},{1,25},{2,26},{3,27},{4,28},{5,29},{6,30},{7,31},{8,0},{9,1... | collective-permute-start | bytes 786440 | tf_op jit(solution)/shard_map/ppermute | solution.py:39
  51.3 9.9 %collective-permute-start.19 = (bf16[2,512,128]{2,1,0:T(8,128)(2,1)S(1)}, bf16[2,512,128]{2,1,0:T(8,128)(2,1)S(1)}, u32[]{:S(2)}, u32[]{:S(2)}) collective-permute-start(bf16[2,512,128]{2,1,0:T(8,128)(2,1)S(1)} %get-tuple-element.126.lo), channel_id=1, source_target_pairs={{0,8},{1,9},{2,10},{3,11},{4,12},{5,13},{6,14},{7,15},{8,16},{9,17... | collective-permute-start | bytes 786440 | tf_op jit(solution)/shard_map/ppermute | solution.py:39
  51.3 15.3 %collective-permute-start.23 = (bf16[2,512,128]{2,1,0:T(8,128)(2,1)S(1)}, bf16[2,512,128]{2,1,0:T(8,128)(2,1)S(1)}, u32[]{:S(2)}, u32[]{:S(2)}) collective-permute-start(bf16[2,512,128]{2,1,0:T(8,128)(2,1)S(1)} %get-tuple-element.126.lo), channel_id=1, source_target_pairs={{0,24},{1,25},{2,26},{3,27},{4,28},{5,29},{6,30},{7,31},{8,0},{9,1... | collective-permute-start | bytes 786440 | tf_op jit(solution)/shard_map/ppermute | solution.py:39
  61.2 7.6 %collective-permute-start.20 = (bf16[2,512,128]{2,1,0:T(8,128)(2,1)S(1)}, bf16[2,512,128]{2,1,0:T(8,128)(2,1)S(1)}, u32[]{:S(2)}, u32[]{:S(2)}) collective-permute-start(bf16[2,512,128]{2,1,0:T(8,128)(2,1)S(1)} %collective-permute-done.19.lo), channel_id=1, source_target_pairs={{0,8},{1,9},{2,10},{3,11},{4,12},{5,13},{6,14},{7,15},{8,16},{9,17... | collective-permute-start | bytes 786440 | tf_op jit(solution)/shard_map/ppermute | solution.py:39
  61.2 7.6 %collective-permute-start.22 = (bf16[2,512,128]{2,1,0:T(8,128)(2,1)S(1)}, bf16[2,512,128]{2,1,0:T(8,128)(2,1)S(1)}, u32[]{:S(2)}, u32[]{:S(2)}) collective-permute-start(bf16[2,512,128]{2,1,0:T(8,128)(2,1)S(1)} %collective-permute-done.21.hi), channel_id=1, source_target_pairs={{0,24},{1,25},{2,26},{3,27},{4,28},{5,29},{6,30},{7,31},{8,0},{9,1... | collective-permute-start | bytes 786440 | tf_op jit(solution)/shard_map/ppermute | solution.py:39
  68.8 2.2 %copy-start.1 = (bf16[512,4096]{1,0:T(8,128)(2,1)S(1)}, bf16[512,4096]{1,0:T(8,128)(2,1)}, u32[]{:S(2)}) copy-start(bf16[512,4096]{1,0:T(8,128)(2,1)} %w.3) | copy-start | bytes 12582916
  73.0 2.7 %collective-permute-start.25 = (bf16[4,256,512]{2,1,0:T(8,128)(2,1)S(1)}, bf16[4,256,512]{2,1,0:T(8,128)(2,1)S(1)}, u32[]{:S(2)}, u32[]{:S(2)}) collective-permute-start(bf16[4,256,512]{2,1,0:T(8,128)(2,1)S(1)} %product.3), channel_id=1, source_target_pairs={{0,32},{32,0},{64,96},{96,64},{128,160},{160,128},{192,224},{224,1... | collective-permute-start | bytes 3145736 | tf_op jit(solution)/shard_map/ppermute | solution.py:57
  75.8 5.6 %collective-permute-start.26 = (bf16[128,512]{1,0:T(8,128)(2,1)S(1)}, bf16[128,512]{1,0:T(8,128)(2,1)S(1)}, u32[]{:S(2)}, u32[]{:S(2)}) collective-permute-start(bf16[128,512]{1,0:T(8,128)(2,1)S(1)} %get-tuple-element.144), channel_id=1, source_target_pairs={{0,64},{32,96},{64,128},{96,160},{128,192},{160,224},{192,0},{224,... | collective-permute-start | bytes 393224 | tf_op jit(solution)/shard_map/ppermute | solution.py:51
  76.3 6.5 %collective-permute-start.27 = (bf16[128,512]{1,0:T(8,128)(2,1)S(1)}, bf16[128,512]{1,0:T(8,128)(2,1)S(1)}, u32[]{:S(2)}, u32[]{:S(2)}) collective-permute-start(bf16[128,512]{1,0:T(8,128)(2,1)S(1)} %get-tuple-element.145), channel_id=1, source_target_pairs={{0,192},{32,224},{64,0},{96,32},{128,64},{160,96},{192,128},{224,1... | collective-permute-start | bytes 393224 | tf_op jit(solution)/shard_map/ppermute | solution.py:51
  82.9 7.3 %collective-permute-start.28 = (bf16[256,512]{1,0:T(8,128)(2,1)S(1)}, bf16[256,512]{1,0:T(8,128)(2,1)S(1)}, u32[]{:S(2)}, u32[]{:S(2)}) collective-permute-start(bf16[256,512]{1,0:T(8,128)(2,1)S(1)} %get-tuple-element.146), channel_id=1, source_target_pairs={{0,64},{32,96},{64,128},{96,160},{128,192},{160,224},{192,0},{224,... | collective-permute-start | bytes 786440 | tf_op jit(solution)/shard_map/ppermute | solution.py:51
  83.5 8.3 %collective-permute-start.29 = (bf16[256,512]{1,0:T(8,128)(2,1)S(1)}, bf16[256,512]{1,0:T(8,128)(2,1)S(1)}, u32[]{:S(2)}, u32[]{:S(2)}) collective-permute-start(bf16[256,512]{1,0:T(8,128)(2,1)S(1)} %get-tuple-element.147), channel_id=1, source_target_pairs={{0,192},{32,224},{64,0},{96,32},{128,64},{160,96},{192,128},{224,1... | collective-permute-start | bytes 786440 | tf_op jit(solution)/shard_map/ppermute | solution.py:51
where the time goes:
time: 93.1 us; the launch traced here: 92.6 us
  starting transfers between devices  36.5 us (39%)
  waiting for transfers between devices  27 us (29%)
  Pallas kernels  20.6 us (22%)
  other arithmetic  2.91 us (3%)
  matrix products  2.67 us (3%)
  between operations  2.31 us (2%)
    ppermute x7, starting transfers between devices, shift_z(): lax.ppermute(block, 'seq', [(y * NZ + z, y * NZ + (z + d) % NZ) for y in...  15.9 us
    ppermute x9, starting transfers between devices, shift_y(): lax.ppermute(block, 'seq', [(y * NZ + z, (y + d) % NY * NZ + z) for y in...  15.1 us
    ppermute x4, waiting for transfers between devices, shift_x(): lax.ppermute(block, 'heads', [(2 * x + c, 2 * ((x + d) % NX) + c) for x i...  11.6 us
    ppermute x2, waiting for transfers between devices, local(): lax.ppermute((key_rows, value_rows), 'seq', route)  7.13 us
    pallas_call x3, Pallas kernels, far(): pl.pallas_call(functools.partial(far_kernel, shift), out_shape=state_shap...  6.39 us
    ppermute x9, waiting for transfers between devices, shift_y(): lax.ppermute(block, 'seq', [(y * NZ + z, (y + d) % NY * NZ + z) for y in...  5.54 us
    ppermute x4, starting transfers between devices, shift_x(): lax.ppermute(block, 'heads', [(2 * x + c, 2 * ((x + d) % NX) + c) for x i...  4.21 us
    pallas_call x2, Pallas kernels, product(): pl.pallas_call(product_kernel, out_shape=jax.ShapeDtypeStruct((NX, rows,...  3.94 us
  transfers between devices with their start and end apart: 23, of which 13 were waited for; matrix products, arithmetic and copies ran while one was open for 4% of the time, Pallas kernels for 11%

commit v1 on v0

--- a/solution.py
+++ b/solution.py
@@ -353,16 +353,18 @@
         ring[4] = shift_z(ring[2], 2)
         return ring
 
-    made = []
+    made, before = [], []
 
     def between(*phase):
         *phase, keys, values, rows_made = tie(*phase, key_rows, value_rows, queries)
         made.extend((keys, values, rows_made))
+        phase[1], *arrived = tie(phase[1], *lax.ppermute((key_rows, value_rows), "seq", route))
+        before.extend(arrived)
         return phase
 
     ring = along_z(column, between)
     key_rows, value_rows, queries = made
-    before_keys, before_values = lax.ppermute((key_rows, value_rows), "seq", route)
+    before_keys, before_values = before
     half = jax.ShapeDtypeStruct((2, 8 * BLK, HD), bf16)
 
     def compact(*sources):
@@ -378,7 +380,6 @@
             )(tab, *sources)
         )
 
-    rest, before_keys, before_values = tie(rest, before_keys, before_values)
     own = lax.cond(
         crowded,
         lambda rest, *ring: compact(*ring, *along_z(rest)),

time: 93.1 us -> 90.8 us (0.975)
  starting transfers between devices: 36.5 us -> 33.7 us
  waiting for transfers between devices: 27 us -> 28.1 us
    ppermute x7, waiting for transfers between devices: 2.01 us -> 6.82 us  [shift_z(): lax.ppermute(block, 'seq', [(y * NZ + z, y * NZ + (z + d) % NZ) for y in...]
    ppermute x7, starting transfers between devices: 15.9 us -> 12.2 us  [shift_z(): lax.ppermute(block, 'seq', [(y * NZ + z, y * NZ + (z + d) % NZ) for y in...]
    ppermute x2, waiting for transfers between devices: 7.13 us -> 4.54 us  [between(): lax.ppermute((key_rows, value_rows), 'seq', route)]
    ppermute x9, waiting for transfers between devices: 5.54 us -> 4.42 us  [shift_y(): lax.ppermute(block, 'seq', [(y * NZ + z, (y + d) % NY * NZ + z) for y in...]
  transfers between devices with their start and end apart: 23 -> 23, of which waited for: 13 -> 15; matrix products, arithmetic and copies ran while one was open for 4% -> 4% of each run, Pallas kernels for 11% -> 12%
where the time goes in v1:
time: 90.8 us; the launch traced here: 90.3 us
  starting transfers between devices  33.7 us (37%)
  waiting for transfers between devices  28.1 us (31%)
  Pallas kernels  20.5 us (23%)
  other arithmetic  2.91 us (3%)
  matrix products  2.67 us (3%)
  between operations  2.31 us (3%)
    ppermute x9, starting transfers between devices, shift_y(): lax.ppermute(block, 'seq', [(y * NZ + z, (y + d) % NY * NZ + z) for y in...  15.1 us
    ppermute x7, starting transfers between devices, shift_z(): lax.ppermute(block, 'seq', [(y * NZ + z, y * NZ + (z + d) % NZ) for y in...  12.2 us
    ppermute x4, waiting for transfers between devices, shift_x(): lax.ppermute(block, 'heads', [(2 * x + c, 2 * ((x + d) % NX) + c) for x i...  11.6 us
    ppermute x7, waiting for transfers between devices, shift_z(): lax.ppermute(block, 'seq', [(y * NZ + z, y * NZ + (z + d) % NZ) for y in...  6.82 us
    pallas_call x3, Pallas kernels, far(): pl.pallas_call(functools.partial(far_kernel, shift), out_shape=state_shap...  6.39 us
    ppermute x2, waiting for transfers between devices, between(): lax.ppermute((key_rows, value_rows), 'seq', route)  4.54 us
    ppermute x9, waiting for transfers between devices, shift_y(): lax.ppermute(block, 'seq', [(y * NZ + z, (y + d) % NY * NZ + z) for y in...  4.42 us
    ppermute x4, starting transfers between devices, shift_x(): lax.ppermute(block, 'heads', [(2 * x + c, 2 * ((x + d) % NX) + c) for x i...  4.21 us
  transfers between devices with their start and end apart: 23, of which 15 were waited for; matrix products, arithmetic and copies ran while one was open for 4% of the time, Pallas kernels for 12%

profile of v1, /device:TPU:6, one launch (start us, length us, event | category | flops | bytes accessed | tf_op | source)
XLA Modules:
  0.0 90.3 jit_solution(17021679457303099014)
XLA Ops:
  0.8 0.7 compare_select_fusion
  1.9 0.8 compare_reduce_fusion
  2.7 2.4 %pick.1 = (bf16[2,2,64,128]{3,2,1,0:T(8,128)(2,1)}, bf16[2,2,64,128]{3,2,1,0:T(8,128)(2,1)}, bf16[2,2,64,128]{3,2,1,0:T(8,128)(2,1)}, bf16[2,2,64,128]{3,2,1,0:T(8,128)(2,1)}) custom-call(s32[128]{0:T(128)S(1)} %compare_select_fusion.1.tab, bf16[1,1024,128]{2,1,0:T(8,128)(2,1)} %ck.1, bf16[1,1024,128]{2,1,0:T(8,128)(2,1)} %cv.1), custom_call_target="tpu_custom_call" | custom-call | flops 700000000 | tf_op jit(solution)/shard_map/pick/pallas_call | solution.py:314
  5.1 3.1 %collective-permute-start.9 = (bf16[2,2,64,128]{3,2,1,0:T(8,128)(2,1)}, bf16[2,2,64,128]{3,2,1,0:T(8,128)(2,1)S(1)}, u32[]{:S(2)}, u32[]{:S(2)}) collective-permute-start(bf16[2,2,64,128]{3,2,1,0:T(8,128)(2,1)} %get-tuple-element.110), channel_id=1, source_target_pairs={{0,24},{1,25},{2,26},{3,27},{4,28},{5,29},{6,30},{7,31},{8,0},{9,1... | collective-permute-start | bytes 196616 | tf_op jit(solution)/shard_map/ppermute | solution.py:39
  8.2 2.2 %collective-permute-start.8 = (bf16[2,2,64,128]{3,2,1,0:T(8,128)(2,1)}, bf16[2,2,64,128]{3,2,1,0:T(8,128)(2,1)S(1)}, u32[]{:S(2)}, u32[]{:S(2)}) collective-permute-start(bf16[2,2,64,128]{3,2,1,0:T(8,128)(2,1)} %get-tuple-element.109), channel_id=1, source_target_pairs={{0,16},{1,17},{2,18},{3,19},{4,20},{5,21},{6,22},{7,23},{8,24},{9,... | collective-permute-start | bytes 196616 | tf_op jit(solution)/shard_map/ppermute | solution.py:39
  10.4 0.5 fusion
  10.9 0.6 fusion.2
  11.6 3.1 %collective-permute-done.7.r1 = bf16[2,2,64,128]{3,2,1,0:T(8,128)(2,1)S(1)} collective-permute-done((bf16[2,2,64,128]{3,2,1,0:T(8,128)(2,1)}, bf16[2,2,64,128]{3,2,1,0:T(8,128)(2,1)S(1)}, u32[]{:S(2)}, u32[]{:S(2)}) %collective-permute-start.7) | collective-permute-done | bytes 65568 | tf_op jit(solution)/shard_map/ppermute | solution.py:39
  14.7 0.9 column.1
  15.6 3.3 %collective-permute-start.10 = (bf16[4,2,64,128]{3,2,1,0:T(8,128)(2,1)S(1)}, bf16[4,2,64,128]{3,2,1,0:T(8,128)(2,1)S(1)}, u32[]{:S(2)}, u32[]{:S(2)}) collective-permute-start(bf16[4,2,64,128]{3,2,1,0:T(8,128)(2,1)S(1)} %get-tuple-element.112), channel_id=1, source_target_pairs={{0,2},{1,3},{2,4},{3,5},{4,6},{5,7},{6,0},{7,1},{8,10},{9,11},{10,... | collective-permute-start | bytes 393224 | tf_op jit(solution)/shard_map/ppermute | solution.py:45
  18.9 3.1 %collective-permute-start.11 = (bf16[4,2,64,128]{3,2,1,0:T(8,128)(2,1)S(1)}, bf16[4,2,64,128]{3,2,1,0:T(8,128)(2,1)S(1)}, u32[]{:S(2)}, u32[]{:S(2)}) collective-permute-start(bf16[4,2,64,128]{3,2,1,0:T(8,128)(2,1)S(1)} %get-tuple-element.112), channel_id=1, source_target_pairs={{0,6},{1,7},{2,0},{3,1},{4,2},{5,3},{6,4},{7,5},{8,14},{9,15},{10,... | collective-permute-start | bytes 393224 | tf_op jit(solution)/shard_map/ppermute | solution.py:45
  22.0 1.0 %collective-permute-start.12 = (bf16[4,2,64,128]{3,2,1,0:T(8,128)(2,1)S(1)}, bf16[4,2,64,128]{3,2,1,0:T(8,128)(2,1)S(1)}, u32[]{:S(2)}, u32[]{:S(2)}) collective-permute-start(bf16[4,2,64,128]{3,2,1,0:T(8,128)(2,1)S(1)} %get-tuple-element.112), channel_id=1, source_target_pairs={{0,1},{1,2},{2,3},{3,4},{4,5},{5,6},{6,7},{7,0},{8,9},{9,10},{10,1... | collective-permute-start | bytes 393224 | tf_op jit(solution)/shard_map/ppermute | solution.py:45
  23.0 2.2 %collective-permute-start.13 = (bf16[4,2,64,128]{3,2,1,0:T(8,128)(2,1)S(1)}, bf16[4,2,64,128]{3,2,1,0:T(8,128)(2,1)S(1)}, u32[]{:S(2)}, u32[]{:S(2)}) collective-permute-start(bf16[4,2,64,128]{3,2,1,0:T(8,128)(2,1)S(1)} %get-tuple-element.112), channel_id=1, source_target_pairs={{0,7},{1,0},{2,1},{3,2},{4,3},{5,4},{6,5},{7,6},{8,15},{9,8},{10,9... | collective-permute-start | bytes 393224 | tf_op jit(solution)/shard_map/ppermute | solution.py:45
  25.3 0.7 convolution_convert_fusion.1.v
  26.0 0.7 convolution_convert_fusion.2.k
  26.8 1.9 %collective-permute-start.17 = (bf16[256,128]{1,0:T(8,128)(2,1)S(1)}, bf16[256,128]{1,0:T(8,128)(2,1)S(1)}, u32[]{:S(2)}, u32[]{:S(2)}) collective-permute-start(bf16[256,128]{1,0:T(8,128)(2,1)S(1)} %convolution_convert_fusion.1.v), channel_id=1, source_target_pairs={{0,1},{1,2},{2,3},{3,4},{4,5},{5,6},{6,7},{7,8},{8,9},{9,10},{10,1... | collective-permute-start | bytes 196616 | tf_op jit(solution)/shard_map/ppermute | solution.py:361
  28.8 1.2 %convolution_convert_fusion.q = bf16[256,512]{1,0:T(8,128)(2,1)S(1)} fusion(bf16[256,4096]{1,0:T(8,128)(2,1)S(1)} %fusion.2, bf16[4096,512]{1,0:T(8,128)(2,1)S(1)} %copy-done.7), kind=kOutput, calls=%fused_computation.5 | convolution fusion | flops 1073872896 | bytes 6553600 | tf_op jit(solution)/shard_map/dot_general | solution.py:344
  30.1 0.4 collective-permute-done.13
  30.5 3.8 %collective-permute-done.16.kp = bf16[256,128]{1,0:T(8,128)(2,1)S(1)} collective-permute-done((bf16[256,128]{1,0:T(8,128)(2,1)S(1)}, bf16[256,128]{1,0:T(8,128)(2,1)S(1)}, u32[]{:S(2)}, u32[]{:S(2)}) %collective-permute-start.16) | collective-permute-done | bytes 65568 | tf_op jit(solution)/shard_map/ppermute | solution.py:361
  34.4 0.7 collective-permute-done.17.vp
  35.1 2.0 %collective-permute-start.14 = (bf16[4,2,64,128]{3,2,1,0:T(8,128)(2,1)S(1)}, bf16[4,2,64,128]{3,2,1,0:T(8,128)(2,1)S(1)}, u32[]{:S(2)}, u32[]{:S(2)}) collective-permute-start(bf16[4,2,64,128]{3,2,1,0:T(8,128)(2,1)S(1)} %collective-permute-done.10), channel_id=1, source_target_pairs={{0,1},{1,2},{2,3},{3,4},{4,5},{5,6},{6,7},{7,0},{8,9},{9,10},{10,1... | collective-permute-start | bytes 393224 | tf_op jit(solution)/shard_map/ppermute | solution.py:45
  37.1 0.5 collective-permute-start.15
  38.9 1.2 %collective-permute-done.18 = bf16[4,2,64,128]{3,2,1,0:T(8,128)(2,1)S(1)} collective-permute-done((bf16[4,2,64,128]{3,2,1,0:T(8,128)(2,1)S(1)}, bf16[4,2,64,128]{3,2,1,0:T(8,128)(2,1)S(1)}, u32[]{:S(2)}, u32[]{:S(2)}) %collective-permute-start.18) | collective-permute-done | bytes 131104 | tf_op jit(solution)/shard_map/ppermute | solution.py:45
  40.1 2.1 %collective-permute-done.14 = bf16[4,2,64,128]{3,2,1,0:T(8,128)(2,1)S(1)} collective-permute-done((bf16[4,2,64,128]{3,2,1,0:T(8,128)(2,1)S(1)}, bf16[4,2,64,128]{3,2,1,0:T(8,128)(2,1)S(1)}, u32[]{:S(2)}, u32[]{:S(2)}) %collective-permute-start.14) | collective-permute-done | bytes 131104 | tf_op jit(solution)/shard_map/ppermute | solution.py:45
  42.2 3.0 %collective-permute-done.15 = bf16[4,2,64,128]{3,2,1,0:T(8,128)(2,1)S(1)} collective-permute-done((bf16[4,2,64,128]{3,2,1,0:T(8,128)(2,1)S(1)}, bf16[4,2,64,128]{3,2,1,0:T(8,128)(2,1)S(1)}, u32[]{:S(2)}, u32[]{:S(2)}) %collective-permute-start.15) | collective-permute-done | bytes 131104 | tf_op jit(solution)/shard_map/ppermute | solution.py:45
  45.2 1.6 %conditional.1 = ((bf16[2,512,128]{2,1,0:T(8,128)(2,1)S(1)}, bf16[2,512,128]{2,1,0:T(8,128)(2,1)S(1)})) conditional(s32[]{:T(128)} %convert_element_type.27, (s32[128]{0:T(128)S(1)}, bf16[4,2,64,128]{3,2,1,0:T(8,128)(2,1)S(1)}, bf16[4,2,64,128]{3,2,1,0:T(8,128)(2,1)S(1)}, bf16[4,2,64,128]{3,2,1,0:T(8,128)(2,1)S(1)}, ...), branch_computations={%region_4.5_spmd, %region_5.6_spmd} | conditional | flops 1300000000 | bytes 3670304 | solution.py:383
  45.2 1.6 %row.2 = (bf16[2,512,128]{2,1,0:T(8,128)(2,1)S(1)}, bf16[2,512,128]{2,1,0:T(8,128)(2,1)S(1)}) custom-call(s32[128]{0:T(128)S(1)} %get-tuple-element.43.tab, bf16[4,2,64,128]{3,2,1,0:T(8,128)(2,1)S(1)} %get-tuple-element.44.refs_0_, bf16[4,2,64,128]{3,2,1,0:T(8,128)(2,1)S(1)} %get-tuple-element.45.refs_1_, ...), custom_call_target="tpu_custom_call" | custom-call | flops 1300000000 | tf_op jit(solution)/shard_map/cond/branch_0_fun/row/pallas_call | solution.py:372
  46.9 3.2 %collective-permute-start.21 = (bf16[2,512,128]{2,1,0:T(8,128)(2,1)S(1)}, bf16[2,512,128]{2,1,0:T(8,128)(2,1)S(1)}, u32[]{:S(2)}, u32[]{:S(2)}) collective-permute-start(bf16[2,512,128]{2,1,0:T(8,128)(2,1)S(1)} %get-tuple-element.125.hi), channel_id=1, source_target_pairs={{0,24},{1,25},{2,26},{3,27},{4,28},{5,29},{6,30},{7,31},{8,0},{9,1... | collective-permute-start | bytes 786440 | tf_op jit(solution)/shard_map/ppermute | solution.py:39
  50.1 3.2 %collective-permute-start.23 = (bf16[2,512,128]{2,1,0:T(8,128)(2,1)S(1)}, bf16[2,512,128]{2,1,0:T(8,128)(2,1)S(1)}, u32[]{:S(2)}, u32[]{:S(2)}) collective-permute-start(bf16[2,512,128]{2,1,0:T(8,128)(2,1)S(1)} %get-tuple-element.124.lo), channel_id=1, source_target_pairs={{0,24},{1,25},{2,26},{3,27},{4,28},{5,29},{6,30},{7,31},{8,0},{9,1... | collective-permute-start | bytes 786440 | tf_op jit(solution)/shard_map/ppermute | solution.py:39
  53.3 2.2 %near.1 = (f32[4,256,128]{2,1,0:T(8,128)S(1)}, f32[4,256,128]{2,1,0:T(8,128)S(1)}, f32[4,256,128]{2,1,0:T(8,128)S(1)}) custom-call(s32[1,4]{1,0:T(1,128)S(1)} %copy-done.2, s32[1]{0:T(128)S(6)} %copy.18.cnt, bf16[256,512]{1,0:T(8,128)(2,1)S(1)} %convolution_convert_fusion.q, bf16[256,128]{1,0:T(8,128)(2,1)S(1)} %collective-permute-done.16.kp, ...), custom_call_target="tpu_custom_call" | custom-call | flops 2200000000 | tf_op jit(solution)/shard_map/near/pallas_call | solution.py:393
  55.5 2.2 %far.3 = (f32[4,256,128]{2,1,0:T(8,128)S(1)}, f32[4,256,128]{2,1,0:T(8,128)S(1)}, f32[4,256,128]{2,1,0:T(8,128)S(1)}) custom-call(s32[128]{0:T(128)S(1)} %compare_select_fusion.1.tab, bf16[256,512]{1,0:T(8,128)(2,1)S(1)} %convolution_convert_fusion.q, bf16[2,512,128]{2,1,0:T(8,128)(2,1)S(1)} %get-tuple-element.124.lo, ...), custom_call_target="tpu_custom_call" | custom-call | flops 1800000000 | tf_op jit(solution)/shard_map/far/pallas_call | solution.py:404
  57.7 1.2 %collective-permute-done.19.lo = bf16[2,512,128]{2,1,0:T(8,128)(2,1)S(1)} collective-permute-done((bf16[2,512,128]{2,1,0:T(8,128)(2,1)S(1)}, bf16[2,512,128]{2,1,0:T(8,128)(2,1)S(1)}, u32[]{:S(2)}, u32[]{:S(2)}) %collective-permute-start.19) | collective-permute-done | bytes 262176 | tf_op jit(solution)/shard_map/ppermute | solution.py:39
  58.9 3.2 %collective-permute-start.22 = (bf16[2,512,128]{2,1,0:T(8,128)(2,1)S(1)}, bf16[2,512,128]{2,1,0:T(8,128)(2,1)S(1)}, u32[]{:S(2)}, u32[]{:S(2)}) collective-permute-start(bf16[2,512,128]{2,1,0:T(8,128)(2,1)S(1)} %collective-permute-done.21.hi), channel_id=1, source_target_pairs={{0,24},{1,25},{2,26},{3,27},{4,28},{5,29},{6,30},{7,31},{8,0},{9,1... | collective-permute-start | bytes 786440 | tf_op jit(solution)/shard_map/ppermute | solution.py:39
  62.2 2.1 %far.4 = (f32[4,256,128]{2,1,0:T(8,128)S(1)}, f32[4,256,128]{2,1,0:T(8,128)S(1)}, f32[4,256,128]{2,1,0:T(8,128)S(1)}) custom-call(s32[128]{0:T(128)S(1)} %compare_select_fusion.1.tab, bf16[256,512]{1,0:T(8,128)(2,1)S(1)} %convolution_convert_fusion.q, bf16[2,512,128]{2,1,0:T(8,128)(2,1)S(1)} %collective-permute-done.19.lo, ...), custom_call_target="tpu_custom_call" | custom-call | flops 1800000000 | tf_op jit(solution)/shard_map/far/pallas_call | solution.py:404
  64.3 2.1 %far.5 = (f32[4,256,128]{2,1,0:T(8,128)S(1)}, f32[4,256,128]{2,1,0:T(8,128)S(1)}, f32[4,256,128]{2,1,0:T(8,128)S(1)}) custom-call(s32[128]{0:T(128)S(1)} %compare_select_fusion.1.tab, bf16[256,512]{1,0:T(8,128)(2,1)S(1)} %convolution_convert_fusion.q, bf16[2,512,128]{2,1,0:T(8,128)(2,1)S(1)} %collective-permute-done.23.lo, ...), custom_call_target="tpu_custom_call" | custom-call | flops 1800000000 | tf_op jit(solution)/shard_map/far/pallas_call | solution.py:404
  66.5 2.2 %last.1.att = bf16[256,512]{1,0:T(8,128)(2,1)S(1)} custom-call(s32[128]{0:T(128)S(1)} %compare_select_fusion.1.tab, bf16[256,512]{1,0:T(8,128)(2,1)S(1)} %convolution_convert_fusion.q, bf16[2,512,128]{2,1,0:T(8,128)(2,1)S(1)} %collective-permute-done.20.lo, bf16[2,512,128]{2,1,0:T(8,128)(2,1)S(1)} %collective-permute-done.22.hi, ...), custom_call_target="tpu_custom_call" | custom-call | flops 2500000000 | tf_op jit(solution)/shard_map/last/pallas_call | solution.py:420
  68.7 2.0 %product.3 = bf16[4,256,512]{2,1,0:T(8,128)(2,1)S(1)} custom-call(s32[4]{0:T(128)S(1)} %get-tuple-element.143.cols, bf16[256,512]{1,0:T(8,128)(2,1)S(1)} %last.1.att, bf16[512,4096]{1,0:T(8,128)(2,1)S(1)} %copy-done.1), custom_call_target="tpu_custom_call" | custom-call | flops 2000000000 | tf_op jit(solution)/shard_map/product/pallas_call | solution.py:433
  70.8 2.0 %product.2.mine = f32[4,256,512]{2,1,0:T(8,128)S(1)} custom-call(s32[4]{0:T(128)S(1)} %get-tuple-element.105.cols, bf16[256,512]{1,0:T(8,128)(2,1)S(1)} %last.1.att, bf16[512,4096]{1,0:T(8,128)(2,1)S(1)} %copy-done.1), custom_call_target="tpu_custom_call" | custom-call | flops 2000000000 | tf_op jit(solution)/shard_map/product/pallas_call | solution.py:433
  72.8 0.7 collective-permute-done.25.recv
  73.5 0.6 collective-permute-start.26
  74.1 1.5 %collective-permute-start.27 = (bf16[128,512]{1,0:T(8,128)(2,1)S(1)}, bf16[128,512]{1,0:T(8,128)(2,1)S(1)}, u32[]{:S(2)}, u32[]{:S(2)}) collective-permute-start(bf16[128,512]{1,0:T(8,128)(2,1)S(1)} %get-tuple-element.145), channel_id=1, source_target_pairs={{0,192},{32,224},{64,0},{96,32},{128,64},{160,96},{192,128},{224,1... | collective-permute-start | bytes 393224 | tf_op jit(solution)/shard_map/ppermute | solution.py:51
  75.6 3.5 %collective-permute-done.26.a = bf16[128,512]{1,0:T(8,128)(2,1)S(1)} collective-permute-done((bf16[128,512]{1,0:T(8,128)(2,1)S(1)}, bf16[128,512]{1,0:T(8,128)(2,1)S(1)}, u32[]{:S(2)}, u32[]{:S(2)}) %collective-permute-start.26) | collective-permute-done | bytes 131104 | tf_op jit(solution)/shard_map/ppermute | solution.py:51
  79.1 1.4 %collective-permute-done.27.b = bf16[128,512]{1,0:T(8,128)(2,1)S(1)} collective-permute-done((bf16[128,512]{1,0:T(8,128)(2,1)S(1)}, bf16[128,512]{1,0:T(8,128)(2,1)S(1)}, u32[]{:S(2)}, u32[]{:S(2)}) %collective-permute-start.27) | collective-permute-done | bytes 131104 | tf_op jit(solution)/shard_map/ppermute | solution.py:51
  80.7 0.4 collective-permute-start.28
  81.1 1.7 %collective-permute-start.29 = (bf16[256,512]{1,0:T(8,128)(2,1)S(1)}, bf16[256,512]{1,0:T(8,128)(2,1)S(1)}, u32[]{:S(2)}, u32[]{:S(2)}) collective-permute-start(bf16[256,512]{1,0:T(8,128)(2,1)S(1)} %get-tuple-element.147), channel_id=1, source_target_pairs={{0,192},{32,224},{64,0},{96,32},{128,64},{160,96},{192,128},{224,1... | collective-permute-start | bytes 786440 | tf_op jit(solution)/shard_map/ppermute | solution.py:51
  82.8 5.2 %collective-permute-done.28.a = bf16[256,512]{1,0:T(8,128)(2,1)S(1)} collective-permute-done((bf16[256,512]{1,0:T(8,128)(2,1)S(1)}, bf16[256,512]{1,0:T(8,128)(2,1)S(1)}, u32[]{:S(2)}, u32[]{:S(2)}) %collective-permute-start.28) | collective-permute-done | bytes 262176 | tf_op jit(solution)/shard_map/ppermute | solution.py:51
  88.0 1.5 %collective-permute-done.29.b = bf16[256,512]{1,0:T(8,128)(2,1)S(1)} collective-permute-done((bf16[256,512]{1,0:T(8,128)(2,1)S(1)}, bf16[256,512]{1,0:T(8,128)(2,1)S(1)}, u32[]{:S(2)}, u32[]{:S(2)}) %collective-permute-start.29) | collective-permute-done | bytes 262176 | tf_op jit(solution)/shard_map/ppermute | solution.py:51
  89.5 0.8 final.1
  (44 shorter events, 1.1 us)
Async XLA Ops:
  0.0 25.3 %copy-start = (bf16[4096,128]{1,0:T(8,128)(2,1)S(1)}, bf16[4096,128]{1,0:T(8,128)(2,1)}, u32[]{:S(2)}) copy-start(bf16[4096,128]{1,0:T(8,128)(2,1)} %param.18) | copy-start | bytes 3145732
  0.0 10.4 %copy-start.4 = (bf16[256,4096]{1,0:T(8,128)(2,1)S(1)}, bf16[256,4096]{1,0:T(8,128)(2,1)}, u32[]{:S(2)}) copy-start(bf16[256,4096]{1,0:T(8,128)(2,1)} %param.14) | copy-start | bytes 6291460
  2.7 8.2 %copy-start.6 = (f32[4096]{0:T(1024)S(1)}, f32[4096]{0:T(1024)}, u32[]{:S(2)}) copy-start(f32[4096]{0:T(1024)} %param.15) | copy-start | bytes 49156
  5.1 6.5 %collective-permute-start.9 = (bf16[2,2,64,128]{3,2,1,0:T(8,128)(2,1)}, bf16[2,2,64,128]{3,2,1,0:T(8,128)(2,1)S(1)}, u32[]{:S(2)}, u32[]{:S(2)}) collective-permute-start(bf16[2,2,64,128]{3,2,1,0:T(8,128)(2,1)} %get-tuple-element.110), channel_id=1, source_target_pairs={{0,24},{1,25},{2,26},{3,27},{4,28},{5,29},{6,30},{7,31},{8,0},{9,1... | collective-permute-start | bytes 196616 | tf_op jit(solution)/shard_map/ppermute | solution.py:39
  8.2 6.5 %collective-permute-start.7 = (bf16[2,2,64,128]{3,2,1,0:T(8,128)(2,1)}, bf16[2,2,64,128]{3,2,1,0:T(8,128)(2,1)S(1)}, u32[]{:S(2)}, u32[]{:S(2)}) collective-permute-start(bf16[2,2,64,128]{3,2,1,0:T(8,128)(2,1)} %get-tuple-element.108), channel_id=1, source_target_pairs={{0,8},{1,9},{2,10},{3,11},{4,12},{5,13},{6,14},{7,15},{8,16},{9,17... | collective-permute-start | bytes 196616 | tf_op jit(solution)/shard_map/ppermute | solution.py:39
  8.2 6.5 %collective-permute-start.8 = (bf16[2,2,64,128]{3,2,1,0:T(8,128)(2,1)}, bf16[2,2,64,128]{3,2,1,0:T(8,128)(2,1)S(1)}, u32[]{:S(2)}, u32[]{:S(2)}) collective-permute-start(bf16[2,2,64,128]{3,2,1,0:T(8,128)(2,1)} %get-tuple-element.109), channel_id=1, source_target_pairs={{0,16},{1,17},{2,18},{3,19},{4,20},{5,21},{6,22},{7,23},{8,24},{9,... | collective-permute-start | bytes 196616 | tf_op jit(solution)/shard_map/ppermute | solution.py:39
  10.9 3.7 %copy-start.3 = (bf16[2,2,64,128]{3,2,1,0:T(8,128)(2,1)S(1)}, bf16[2,2,64,128]{3,2,1,0:T(8,128)(2,1)}, u32[]{:S(2)}) copy-start(bf16[2,2,64,128]{3,2,1,0:T(8,128)(2,1)} %get-tuple-element.107.r0) | copy-start | bytes 196612
  15.5 10.4 %copy-start.5 = (bf16[4096,128]{1,0:T(8,128)(2,1)S(1)}, bf16[4096,128]{1,0:T(8,128)(2,1)}, u32[]{:S(2)}) copy-start(bf16[4096,128]{1,0:T(8,128)(2,1)} %param.17) | copy-start | bytes 3145732
  15.6 11.3 %collective-permute-start.10 = (bf16[4,2,64,128]{3,2,1,0:T(8,128)(2,1)S(1)}, bf16[4,2,64,128]{3,2,1,0:T(8,128)(2,1)S(1)}, u32[]{:S(2)}, u32[]{:S(2)}) collective-permute-start(bf16[4,2,64,128]{3,2,1,0:T(8,128)(2,1)S(1)} %get-tuple-element.112), channel_id=1, source_target_pairs={{0,2},{1,3},{2,4},{3,5},{4,6},{5,7},{6,0},{7,1},{8,10},{9,11},{10,... | collective-permute-start | bytes 393224 | tf_op jit(solution)/shard_map/ppermute | solution.py:45
  18.9 11.1 %collective-permute-start.11 = (bf16[4,2,64,128]{3,2,1,0:T(8,128)(2,1)S(1)}, bf16[4,2,64,128]{3,2,1,0:T(8,128)(2,1)S(1)}, u32[]{:S(2)}, u32[]{:S(2)}) collective-permute-start(bf16[4,2,64,128]{3,2,1,0:T(8,128)(2,1)S(1)} %get-tuple-element.112), channel_id=1, source_target_pairs={{0,6},{1,7},{2,0},{3,1},{4,2},{5,3},{6,4},{7,5},{8,14},{9,15},{10,... | collective-permute-start | bytes 393224 | tf_op jit(solution)/shard_map/ppermute | solution.py:45
  22.0 8.1 %collective-permute-start.12 = (bf16[4,2,64,128]{3,2,1,0:T(8,128)(2,1)S(1)}, bf16[4,2,64,128]{3,2,1,0:T(8,128)(2,1)S(1)}, u32[]{:S(2)}, u32[]{:S(2)}) collective-permute-start(bf16[4,2,64,128]{3,2,1,0:T(8,128)(2,1)S(1)} %get-tuple-element.112), channel_id=1, source_target_pairs={{0,1},{1,2},{2,3},{3,4},{4,5},{5,6},{6,7},{7,0},{8,9},{9,10},{10,1... | collective-permute-start | bytes 393224 | tf_op jit(solution)/shard_map/ppermute | solution.py:45
  23.0 7.5 %collective-permute-start.13 = (bf16[4,2,64,128]{3,2,1,0:T(8,128)(2,1)S(1)}, bf16[4,2,64,128]{3,2,1,0:T(8,128)(2,1)S(1)}, u32[]{:S(2)}, u32[]{:S(2)}) collective-permute-start(bf16[4,2,64,128]{3,2,1,0:T(8,128)(2,1)S(1)} %get-tuple-element.112), channel_id=1, source_target_pairs={{0,7},{1,0},{2,1},{3,2},{4,3},{5,4},{6,5},{7,6},{8,15},{9,8},{10,9... | collective-permute-start | bytes 393224 | tf_op jit(solution)/shard_map/ppermute | solution.py:45
  25.3 3.5 %copy-start.7 = (bf16[4096,512]{1,0:T(8,128)(2,1)S(1)}, bf16[4096,512]{1,0:T(8,128)(2,1)}, u32[]{:S(2)}) copy-start(bf16[4096,512]{1,0:T(8,128)(2,1)} %param.16) | copy-start | bytes 12582916
  26.7 7.7 %collective-permute-start.16 = (bf16[256,128]{1,0:T(8,128)(2,1)S(1)}, bf16[256,128]{1,0:T(8,128)(2,1)S(1)}, u32[]{:S(2)}, u32[]{:S(2)}) collective-permute-start(bf16[256,128]{1,0:T(8,128)(2,1)S(1)} %convolution_convert_fusion.2.k), channel_id=1, source_target_pairs={{0,1},{1,2},{2,3},{3,4},{4,5},{5,6},{6,7},{7,8},{8,9},{9,10},{10,1... | collective-permute-start | bytes 196616 | tf_op jit(solution)/shard_map/ppermute | solution.py:361
  26.8 8.3 %collective-permute-start.17 = (bf16[256,128]{1,0:T(8,128)(2,1)S(1)}, bf16[256,128]{1,0:T(8,128)(2,1)S(1)}, u32[]{:S(2)}, u32[]{:S(2)}) collective-permute-start(bf16[256,128]{1,0:T(8,128)(2,1)S(1)} %convolution_convert_fusion.1.v), channel_id=1, source_target_pairs={{0,1},{1,2},{2,3},{3,4},{4,5},{5,6},{6,7},{7,8},{8,9},{9,10},{10,1... | collective-permute-start | bytes 196616 | tf_op jit(solution)/shard_map/ppermute | solution.py:361
  35.1 5.0 %collective-permute-start.18 = (bf16[4,2,64,128]{3,2,1,0:T(8,128)(2,1)S(1)}, bf16[4,2,64,128]{3,2,1,0:T(8,128)(2,1)S(1)}, u32[]{:S(2)}, u32[]{:S(2)}) collective-permute-start(bf16[4,2,64,128]{3,2,1,0:T(8,128)(2,1)S(1)} %collective-permute-done.11), channel_id=1, source_target_pairs={{0,7},{1,0},{2,1},{3,2},{4,3},{5,4},{6,5},{7,6},{8,15},{9,8},{10,9... | collective-permute-start | bytes 393224 | tf_op jit(solution)/shard_map/ppermute | solution.py:45
  35.1 7.1 %collective-permute-start.14 = (bf16[4,2,64,128]{3,2,1,0:T(8,128)(2,1)S(1)}, bf16[4,2,64,128]{3,2,1,0:T(8,128)(2,1)S(1)}, u32[]{:S(2)}, u32[]{:S(2)}) collective-permute-start(bf16[4,2,64,128]{3,2,1,0:T(8,128)(2,1)S(1)} %collective-permute-done.10), channel_id=1, source_target_pairs={{0,1},{1,2},{2,3},{3,4},{4,5},{5,6},{6,7},{7,0},{8,9},{9,10},{10,1... | collective-permute-start | bytes 393224 | tf_op jit(solution)/shard_map/ppermute | solution.py:45
  37.1 8.1 %collective-permute-start.15 = (bf16[4,2,64,128]{3,2,1,0:T(8,128)(2,1)S(1)}, bf16[4,2,64,128]{3,2,1,0:T(8,128)(2,1)S(1)}, u32[]{:S(2)}, u32[]{:S(2)}) collective-permute-start(bf16[4,2,64,128]{3,2,1,0:T(8,128)(2,1)S(1)} %collective-permute-done.10), channel_id=1, source_target_pairs={{0,2},{1,3},{2,4},{3,5},{4,6},{5,7},{6,0},{7,1},{8,10},{9,11},{10,... | collective-permute-start | bytes 393224 | tf_op jit(solution)/shard_map/ppermute | solution.py:45
  45.2 8.1 %copy-start.2 = (s32[1,4]{1,0:T(1,128)S(1)}, s32[1,4]{1,0:T(1,128)}, u32[]{:S(2)}) copy-start(s32[1,4]{1,0:T(1,128)} %offs.1) | copy-start | bytes 52
  46.8 15.4 %collective-permute-start.24 = (bf16[2,512,128]{2,1,0:T(8,128)(2,1)S(1)}, bf16[2,512,128]{2,1,0:T(8,128)(2,1)S(1)}, u32[]{:S(2)}, u32[]{:S(2)}) collective-permute-start(bf16[2,512,128]{2,1,0:T(8,128)(2,1)S(1)} %get-tuple-element.125.hi), channel_id=1, source_target_pairs={{0,8},{1,9},{2,10},{3,11},{4,12},{5,13},{6,14},{7,15},{8,16},{9,17... | collective-permute-start | bytes 786440 | tf_op jit(solution)/shard_map/ppermute | solution.py:39
  46.9 12.1 %collective-permute-start.21 = (bf16[2,512,128]{2,1,0:T(8,128)(2,1)S(1)}, bf16[2,512,128]{2,1,0:T(8,128)(2,1)S(1)}, u32[]{:S(2)}, u32[]{:S(2)}) collective-permute-start(bf16[2,512,128]{2,1,0:T(8,128)(2,1)S(1)} %get-tuple-element.125.hi), channel_id=1, source_target_pairs={{0,24},{1,25},{2,26},{3,27},{4,28},{5,29},{6,30},{7,31},{8,0},{9,1... | collective-permute-start | bytes 786440 | tf_op jit(solution)/shard_map/ppermute | solution.py:39
  50.1 8.9 %collective-permute-start.19 = (bf16[2,512,128]{2,1,0:T(8,128)(2,1)S(1)}, bf16[2,512,128]{2,1,0:T(8,128)(2,1)S(1)}, u32[]{:S(2)}, u32[]{:S(2)}) collective-permute-start(bf16[2,512,128]{2,1,0:T(8,128)(2,1)S(1)} %get-tuple-element.124.lo), channel_id=1, source_target_pairs={{0,8},{1,9},{2,10},{3,11},{4,12},{5,13},{6,14},{7,15},{8,16},{9,17... | collective-permute-start | bytes 786440 | tf_op jit(solution)/shard_map/ppermute | solution.py:39
  50.1 14.2 %collective-permute-start.23 = (bf16[2,512,128]{2,1,0:T(8,128)(2,1)S(1)}, bf16[2,512,128]{2,1,0:T(8,128)(2,1)S(1)}, u32[]{:S(2)}, u32[]{:S(2)}) collective-permute-start(bf16[2,512,128]{2,1,0:T(8,128)(2,1)S(1)} %get-tuple-element.124.lo), channel_id=1, source_target_pairs={{0,24},{1,25},{2,26},{3,27},{4,28},{5,29},{6,30},{7,31},{8,0},{9,1... | collective-permute-start | bytes 786440 | tf_op jit(solution)/shard_map/ppermute | solution.py:39
  58.9 7.6 %collective-permute-start.20 = (bf16[2,512,128]{2,1,0:T(8,128)(2,1)S(1)}, bf16[2,512,128]{2,1,0:T(8,128)(2,1)S(1)}, u32[]{:S(2)}, u32[]{:S(2)}) collective-permute-start(bf16[2,512,128]{2,1,0:T(8,128)(2,1)S(1)} %collective-permute-done.19.lo), channel_id=1, source_target_pairs={{0,8},{1,9},{2,10},{3,11},{4,12},{5,13},{6,14},{7,15},{8,16},{9,17... | collective-permute-start | bytes 786440 | tf_op jit(solution)/shard_map/ppermute | solution.py:39
  58.9 7.6 %collective-permute-start.22 = (bf16[2,512,128]{2,1,0:T(8,128)(2,1)S(1)}, bf16[2,512,128]{2,1,0:T(8,128)(2,1)S(1)}, u32[]{:S(2)}, u32[]{:S(2)}) collective-permute-start(bf16[2,512,128]{2,1,0:T(8,128)(2,1)S(1)} %collective-permute-done.21.hi), channel_id=1, source_target_pairs={{0,24},{1,25},{2,26},{3,27},{4,28},{5,29},{6,30},{7,31},{8,0},{9,1... | collective-permute-start | bytes 786440 | tf_op jit(solution)/shard_map/ppermute | solution.py:39
  66.5 2.2 %copy-start.1 = (bf16[512,4096]{1,0:T(8,128)(2,1)S(1)}, bf16[512,4096]{1,0:T(8,128)(2,1)}, u32[]{:S(2)}) copy-start(bf16[512,4096]{1,0:T(8,128)(2,1)} %w.3) | copy-start | bytes 12582916
  70.7 2.7 %collective-permute-start.25 = (bf16[4,256,512]{2,1,0:T(8,128)(2,1)S(1)}, bf16[4,256,512]{2,1,0:T(8,128)(2,1)S(1)}, u32[]{:S(2)}, u32[]{:S(2)}) collective-permute-start(bf16[4,256,512]{2,1,0:T(8,128)(2,1)S(1)} %product.3), channel_id=1, source_target_pairs={{0,32},{32,0},{64,96},{96,64},{128,160},{160,128},{192,224},{224,1... | collective-permute-start | bytes 3145736 | tf_op jit(solution)/shard_map/ppermute | solution.py:57
  73.5 5.6 %collective-permute-start.26 = (bf16[128,512]{1,0:T(8,128)(2,1)S(1)}, bf16[128,512]{1,0:T(8,128)(2,1)S(1)}, u32[]{:S(2)}, u32[]{:S(2)}) collective-permute-start(bf16[128,512]{1,0:T(8,128)(2,1)S(1)} %get-tuple-element.144), channel_id=1, source_target_pairs={{0,64},{32,96},{64,128},{96,160},{128,192},{160,224},{192,0},{224,... | collective-permute-start | bytes 393224 | tf_op jit(solution)/shard_map/ppermute | solution.py:51
  74.1 6.5 %collective-permute-start.27 = (bf16[128,512]{1,0:T(8,128)(2,1)S(1)}, bf16[128,512]{1,0:T(8,128)(2,1)S(1)}, u32[]{:S(2)}, u32[]{:S(2)}) collective-permute-start(bf16[128,512]{1,0:T(8,128)(2,1)S(1)} %get-tuple-element.145), channel_id=1, source_target_pairs={{0,192},{32,224},{64,0},{96,32},{128,64},{160,96},{192,128},{224,1... | collective-permute-start | bytes 393224 | tf_op jit(solution)/shard_map/ppermute | solution.py:51
  80.7 7.3 %collective-permute-start.28 = (bf16[256,512]{1,0:T(8,128)(2,1)S(1)}, bf16[256,512]{1,0:T(8,128)(2,1)S(1)}, u32[]{:S(2)}, u32[]{:S(2)}) collective-permute-start(bf16[256,512]{1,0:T(8,128)(2,1)S(1)} %get-tuple-element.146), channel_id=1, source_target_pairs={{0,64},{32,96},{64,128},{96,160},{128,192},{160,224},{192,0},{224,... | collective-permute-start | bytes 786440 | tf_op jit(solution)/shard_map/ppermute | solution.py:51
  81.1 8.4 %collective-permute-start.29 = (bf16[256,512]{1,0:T(8,128)(2,1)S(1)}, bf16[256,512]{1,0:T(8,128)(2,1)S(1)}, u32[]{:S(2)}, u32[]{:S(2)}) collective-permute-start(bf16[256,512]{1,0:T(8,128)(2,1)S(1)} %get-tuple-element.147), channel_id=1, source_target_pairs={{0,192},{32,224},{64,0},{96,32},{128,64},{160,96},{192,128},{224,1... | collective-permute-start | bytes 786440 | tf_op jit(solution)/shard_map/ppermute | solution.py:51

commit v2 on v1

--- a/solution.py
+++ b/solution.py
@@ -412,7 +412,8 @@
         )(tab, queries, *part, *state)
 
     lo1, hi3 = shift_y(own[0], 1), shift_y(own[1], -1)
-    hi1, lo3 = shift_y(own[1], 1), shift_y(own[0], -1)
+    late_lo, late_hi, *state = tie(*own, *state)
+    hi1, lo3 = shift_y(late_hi, 1), shift_y(late_lo, -1)
     state = far(0, own, state)
     lo2, hi2 = shift_y(lo1, 1), shift_y(hi3, -1)
     state = far(1, (lo1, hi1), state)

time: 90.8 us -> 90.7 us (level)
  transfers between devices with their start and end apart: 23 -> 23, of which waited for: 15 -> 14; matrix products, arithmetic and copies ran while one was open for 4% -> 4% of each run, Pallas kernels for 12% -> 12%
where the time goes in v2:
time: 90.7 us; the launch traced here: 90.5 us
  starting transfers between devices  33.9 us (37%)
  waiting for transfers between devices  28 us (31%)
  Pallas kernels  20.5 us (23%)
  other arithmetic  2.91 us (3%)
  matrix products  2.67 us (3%)
  between operations  2.35 us (3%)
    ppermute x9, starting transfers between devices, shift_y(): lax.ppermute(block, 'seq', [(y * NZ + z, (y + d) % NY * NZ + z) for y in...  15.4 us
    ppermute x7, starting transfers between devices, shift_z(): lax.ppermute(block, 'seq', [(y * NZ + z, y * NZ + (z + d) % NZ) for y in...  12.1 us
    ppermute x4, waiting for transfers between devices, shift_x(): lax.ppermute(block, 'heads', [(2 * x + c, 2 * ((x + d) % NX) + c) for x i...  11.8 us
    ppermute x7, waiting for transfers between devices, shift_z(): lax.ppermute(block, 'seq', [(y * NZ + z, y * NZ + (z + d) % NZ) for y in...  6.82 us
    pallas_call x3, Pallas kernels, far(): pl.pallas_call(functools.partial(far_kernel, shift), out_shape=state_shap...  6.39 us
    ppermute x2, waiting for transfers between devices, between(): lax.ppermute((key_rows, value_rows), 'seq', route)  4.55 us
    ppermute x4, starting transfers between devices, shift_x(): lax.ppermute(block, 'heads', [(2 * x + c, 2 * ((x + d) % NX) + c) for x i...  4.21 us
    ppermute x9, waiting for transfers between devices, shift_y(): lax.ppermute(block, 'seq', [(y * NZ + z, (y + d) % NY * NZ + z) for y in...  4.15 us
  transfers between devices with their start and end apart: 23, of which 14 were waited for; matrix products, arithmetic and copies ran while one was open for 4% of the time, Pallas kernels for 12%

profile of v2, /device:TPU:6, one launch (start us, length us, event | category | flops | bytes accessed | tf_op | source)
XLA Modules:
  0.0 90.5 jit_solution(12173315344320163588)
XLA Ops:
  0.8 0.7 compare_select_fusion
  1.9 0.8 compare_reduce_fusion
  2.7 2.4 %pick.1 = (bf16[2,2,64,128]{3,2,1,0:T(8,128)(2,1)}, bf16[2,2,64,128]{3,2,1,0:T(8,128)(2,1)}, bf16[2,2,64,128]{3,2,1,0:T(8,128)(2,1)}, bf16[2,2,64,128]{3,2,1,0:T(8,128)(2,1)}) custom-call(s32[128]{0:T(128)S(1)} %compare_select_fusion.1.tab, bf16[1,1024,128]{2,1,0:T(8,128)(2,1)} %ck.1, bf16[1,1024,128]{2,1,0:T(8,128)(2,1)} %cv.1), custom_call_target="tpu_custom_call" | custom-call | flops 700000000 | tf_op jit(solution)/shard_map/pick/pallas_call | solution.py:314
  5.1 3.1 %collective-permute-start.9 = (bf16[2,2,64,128]{3,2,1,0:T(8,128)(2,1)}, bf16[2,2,64,128]{3,2,1,0:T(8,128)(2,1)S(1)}, u32[]{:S(2)}, u32[]{:S(2)}) collective-permute-start(bf16[2,2,64,128]{3,2,1,0:T(8,128)(2,1)} %get-tuple-element.115), channel_id=1, source_target_pairs={{0,24},{1,25},{2,26},{3,27},{4,28},{5,29},{6,30},{7,31},{8,0},{9,1... | collective-permute-start | bytes 196616 | tf_op jit(solution)/shard_map/ppermute | solution.py:39
  8.2 2.2 %collective-permute-start.8 = (bf16[2,2,64,128]{3,2,1,0:T(8,128)(2,1)}, bf16[2,2,64,128]{3,2,1,0:T(8,128)(2,1)S(1)}, u32[]{:S(2)}, u32[]{:S(2)}) collective-permute-start(bf16[2,2,64,128]{3,2,1,0:T(8,128)(2,1)} %get-tuple-element.114), channel_id=1, source_target_pairs={{0,16},{1,17},{2,18},{3,19},{4,20},{5,21},{6,22},{7,23},{8,24},{9,... | collective-permute-start | bytes 196616 | tf_op jit(solution)/shard_map/ppermute | solution.py:39
  10.4 0.5 fusion
  10.9 0.6 fusion.2
  11.6 3.1 %collective-permute-done.7.r1 = bf16[2,2,64,128]{3,2,1,0:T(8,128)(2,1)S(1)} collective-permute-done((bf16[2,2,64,128]{3,2,1,0:T(8,128)(2,1)}, bf16[2,2,64,128]{3,2,1,0:T(8,128)(2,1)S(1)}, u32[]{:S(2)}, u32[]{:S(2)}) %collective-permute-start.7) | collective-permute-done | bytes 65568 | tf_op jit(solution)/shard_map/ppermute | solution.py:39
  14.7 0.9 column.1
  15.6 3.3 %collective-permute-start.10 = (bf16[4,2,64,128]{3,2,1,0:T(8,128)(2,1)S(1)}, bf16[4,2,64,128]{3,2,1,0:T(8,128)(2,1)S(1)}, u32[]{:S(2)}, u32[]{:S(2)}) collective-permute-start(bf16[4,2,64,128]{3,2,1,0:T(8,128)(2,1)S(1)} %get-tuple-element.117), channel_id=1, source_target_pairs={{0,2},{1,3},{2,4},{3,5},{4,6},{5,7},{6,0},{7,1},{8,10},{9,11},{10,... | collective-permute-start | bytes 393224 | tf_op jit(solution)/shard_map/ppermute | solution.py:45
  18.9 3.1 %collective-permute-start.11 = (bf16[4,2,64,128]{3,2,1,0:T(8,128)(2,1)S(1)}, bf16[4,2,64,128]{3,2,1,0:T(8,128)(2,1)S(1)}, u32[]{:S(2)}, u32[]{:S(2)}) collective-permute-start(bf16[4,2,64,128]{3,2,1,0:T(8,128)(2,1)S(1)} %get-tuple-element.117), channel_id=1, source_target_pairs={{0,6},{1,7},{2,0},{3,1},{4,2},{5,3},{6,4},{7,5},{8,14},{9,15},{10,... | collective-permute-start | bytes 393224 | tf_op jit(solution)/shard_map/ppermute | solution.py:45
  22.0 1.0 %collective-permute-start.12 = (bf16[4,2,64,128]{3,2,1,0:T(8,128)(2,1)S(1)}, bf16[4,2,64,128]{3,2,1,0:T(8,128)(2,1)S(1)}, u32[]{:S(2)}, u32[]{:S(2)}) collective-permute-start(bf16[4,2,64,128]{3,2,1,0:T(8,128)(2,1)S(1)} %get-tuple-element.117), channel_id=1, source_target_pairs={{0,1},{1,2},{2,3},{3,4},{4,5},{5,6},{6,7},{7,0},{8,9},{9,10},{10,1... | collective-permute-start | bytes 393224 | tf_op jit(solution)/shard_map/ppermute | solution.py:45
  23.0 2.2 %collective-permute-start.13 = (bf16[4,2,64,128]{3,2,1,0:T(8,128)(2,1)S(1)}, bf16[4,2,64,128]{3,2,1,0:T(8,128)(2,1)S(1)}, u32[]{:S(2)}, u32[]{:S(2)}) collective-permute-start(bf16[4,2,64,128]{3,2,1,0:T(8,128)(2,1)S(1)} %get-tuple-element.117), channel_id=1, source_target_pairs={{0,7},{1,0},{2,1},{3,2},{4,3},{5,4},{6,5},{7,6},{8,15},{9,8},{10,9... | collective-permute-start | bytes 393224 | tf_op jit(solution)/shard_map/ppermute | solution.py:45
  25.3 0.7 convolution_convert_fusion.1.v
  26.0 0.7 convolution_convert_fusion.2.k
  26.8 1.9 %collective-permute-start.17 = (bf16[256,128]{1,0:T(8,128)(2,1)S(1)}, bf16[256,128]{1,0:T(8,128)(2,1)S(1)}, u32[]{:S(2)}, u32[]{:S(2)}) collective-permute-start(bf16[256,128]{1,0:T(8,128)(2,1)S(1)} %convolution_convert_fusion.1.v), channel_id=1, source_target_pairs={{0,1},{1,2},{2,3},{3,4},{4,5},{5,6},{6,7},{7,8},{8,9},{9,10},{10,1... | collective-permute-start | bytes 196616 | tf_op jit(solution)/shard_map/ppermute | solution.py:361
  28.8 1.2 %convolution_convert_fusion.q = bf16[256,512]{1,0:T(8,128)(2,1)S(1)} fusion(bf16[256,4096]{1,0:T(8,128)(2,1)S(1)} %fusion.2, bf16[4096,512]{1,0:T(8,128)(2,1)S(1)} %copy-done.7), kind=kOutput, calls=%fused_computation.5 | convolution fusion | flops 1073872896 | bytes 6553600 | tf_op jit(solution)/shard_map/dot_general | solution.py:344
  30.1 0.4 collective-permute-done.13
  30.5 3.8 %collective-permute-done.16.kp = bf16[256,128]{1,0:T(8,128)(2,1)S(1)} collective-permute-done((bf16[256,128]{1,0:T(8,128)(2,1)S(1)}, bf16[256,128]{1,0:T(8,128)(2,1)S(1)}, u32[]{:S(2)}, u32[]{:S(2)}) %collective-permute-start.16) | collective-permute-done | bytes 65568 | tf_op jit(solution)/shard_map/ppermute | solution.py:361
  34.4 0.7 collective-permute-done.17.vp
  35.1 2.0 %collective-permute-start.14 = (bf16[4,2,64,128]{3,2,1,0:T(8,128)(2,1)S(1)}, bf16[4,2,64,128]{3,2,1,0:T(8,128)(2,1)S(1)}, u32[]{:S(2)}, u32[]{:S(2)}) collective-permute-start(bf16[4,2,64,128]{3,2,1,0:T(8,128)(2,1)S(1)} %collective-permute-done.10), channel_id=1, source_target_pairs={{0,1},{1,2},{2,3},{3,4},{4,5},{5,6},{6,7},{7,0},{8,9},{9,10},{10,1... | collective-permute-start | bytes 393224 | tf_op jit(solution)/shard_map/ppermute | solution.py:45
  37.1 0.4 collective-permute-start.15
  38.8 1.3 %collective-permute-done.18 = bf16[4,2,64,128]{3,2,1,0:T(8,128)(2,1)S(1)} collective-permute-done((bf16[4,2,64,128]{3,2,1,0:T(8,128)(2,1)S(1)}, bf16[4,2,64,128]{3,2,1,0:T(8,128)(2,1)S(1)}, u32[]{:S(2)}, u32[]{:S(2)}) %collective-permute-start.18) | collective-permute-done | bytes 131104 | tf_op jit(solution)/shard_map/ppermute | solution.py:45
  40.1 2.2 %collective-permute-done.14 = bf16[4,2,64,128]{3,2,1,0:T(8,128)(2,1)S(1)} collective-permute-done((bf16[4,2,64,128]{3,2,1,0:T(8,128)(2,1)S(1)}, bf16[4,2,64,128]{3,2,1,0:T(8,128)(2,1)S(1)}, u32[]{:S(2)}, u32[]{:S(2)}) %collective-permute-start.14) | collective-permute-done | bytes 131104 | tf_op jit(solution)/shard_map/ppermute | solution.py:45
  42.2 2.9 %collective-permute-done.15 = bf16[4,2,64,128]{3,2,1,0:T(8,128)(2,1)S(1)} collective-permute-done((bf16[4,2,64,128]{3,2,1,0:T(8,128)(2,1)S(1)}, bf16[4,2,64,128]{3,2,1,0:T(8,128)(2,1)S(1)}, u32[]{:S(2)}, u32[]{:S(2)}) %collective-permute-start.15) | collective-permute-done | bytes 131104 | tf_op jit(solution)/shard_map/ppermute | solution.py:45
  45.1 1.6 %conditional.1 = ((bf16[2,512,128]{2,1,0:T(8,128)(2,1)S(1)}, bf16[2,512,128]{2,1,0:T(8,128)(2,1)S(1)})) conditional(s32[]{:T(128)} %convert_element_type.27, (s32[128]{0:T(128)S(1)}, bf16[4,2,64,128]{3,2,1,0:T(8,128)(2,1)S(1)}, bf16[4,2,64,128]{3,2,1,0:T(8,128)(2,1)S(1)}, bf16[4,2,64,128]{3,2,1,0:T(8,128)(2,1)S(1)}, ...), branch_computations={%region_4.5_spmd, %region_5.6_spmd} | conditional | flops 1300000000 | bytes 3670304 | solution.py:383
  45.1 1.6 %row.2 = (bf16[2,512,128]{2,1,0:T(8,128)(2,1)S(1)}, bf16[2,512,128]{2,1,0:T(8,128)(2,1)S(1)}) custom-call(s32[128]{0:T(128)S(1)} %get-tuple-element.43.tab, bf16[4,2,64,128]{3,2,1,0:T(8,128)(2,1)S(1)} %get-tuple-element.44.refs_0_, bf16[4,2,64,128]{3,2,1,0:T(8,128)(2,1)S(1)} %get-tuple-element.45.refs_1_, ...), custom_call_target="tpu_custom_call" | custom-call | flops 1300000000 | tf_op jit(solution)/shard_map/cond/branch_0_fun/row/pallas_call | solution.py:372
  46.8 3.2 %collective-permute-start.21 = (bf16[2,512,128]{2,1,0:T(8,128)(2,1)S(1)}, bf16[2,512,128]{2,1,0:T(8,128)(2,1)S(1)}, u32[]{:S(2)}, u32[]{:S(2)}) collective-permute-start(bf16[2,512,128]{2,1,0:T(8,128)(2,1)S(1)} %get-tuple-element.140.hi), channel_id=1, source_target_pairs={{0,24},{1,25},{2,26},{3,27},{4,28},{5,29},{6,30},{7,31},{8,0},{9,1... | collective-permute-start | bytes 786440 | tf_op jit(solution)/shard_map/ppermute | solution.py:39
  50.0 2.2 %near.1 = (f32[4,256,128]{2,1,0:T(8,128)S(1)}, f32[4,256,128]{2,1,0:T(8,128)S(1)}, f32[4,256,128]{2,1,0:T(8,128)S(1)}) custom-call(s32[1,4]{1,0:T(1,128)S(1)} %copy-done.2, s32[1]{0:T(128)S(6)} %copy.18.cnt, bf16[256,512]{1,0:T(8,128)(2,1)S(1)} %convolution_convert_fusion.q, bf16[256,128]{1,0:T(8,128)(2,1)S(1)} %collective-permute-done.16.kp, ...), custom_call_target="tpu_custom_call" | custom-call | flops 2200000000 | tf_op jit(solution)/shard_map/near/pallas_call | solution.py:393
  52.3 3.2 %collective-permute-start.23 = (bf16[2,512,128]{2,1,0:T(8,128)(2,1)S(1)}, bf16[2,512,128]{2,1,0:T(8,128)(2,1)S(1)}, u32[]{:S(2)}, u32[]{:S(2)}) collective-permute-start(bf16[2,512,128]{2,1,0:T(8,128)(2,1)S(1)} %get-tuple-element.139.lo), channel_id=1, source_target_pairs={{0,24},{1,25},{2,26},{3,27},{4,28},{5,29},{6,30},{7,31},{8,0},{9,1... | collective-permute-start | bytes 786440 | tf_op jit(solution)/shard_map/ppermute | solution.py:39
  55.5 2.2 %far.3 = (f32[4,256,128]{2,1,0:T(8,128)S(1)}, f32[4,256,128]{2,1,0:T(8,128)S(1)}, f32[4,256,128]{2,1,0:T(8,128)S(1)}) custom-call(s32[128]{0:T(128)S(1)} %compare_select_fusion.1.tab, bf16[256,512]{1,0:T(8,128)(2,1)S(1)} %convolution_convert_fusion.q, bf16[2,512,128]{2,1,0:T(8,128)(2,1)S(1)} %get-tuple-element.139.lo, ...), custom_call_target="tpu_custom_call" | custom-call | flops 1800000000 | tf_op jit(solution)/shard_map/far/pallas_call | solution.py:404
  58.0 3.2 %collective-permute-start.22 = (bf16[2,512,128]{2,1,0:T(8,128)(2,1)S(1)}, bf16[2,512,128]{2,1,0:T(8,128)(2,1)S(1)}, u32[]{:S(2)}, u32[]{:S(2)}) collective-permute-start(bf16[2,512,128]{2,1,0:T(8,128)(2,1)S(1)} %collective-permute-done.21.hi), channel_id=1, source_target_pairs={{0,24},{1,25},{2,26},{3,27},{4,28},{5,29},{6,30},{7,31},{8,0},{9,1... | collective-permute-start | bytes 786440 | tf_op jit(solution)/shard_map/ppermute | solution.py:39
  61.2 1.0 %collective-permute-done.24.hi = bf16[2,512,128]{2,1,0:T(8,128)(2,1)S(1)} collective-permute-done((bf16[2,512,128]{2,1,0:T(8,128)(2,1)S(1)}, bf16[2,512,128]{2,1,0:T(8,128)(2,1)S(1)}, u32[]{:S(2)}, u32[]{:S(2)}) %collective-permute-start.24) | collective-permute-done | bytes 262176 | tf_op jit(solution)/shard_map/ppermute | solution.py:39
  62.2 2.1 %far.4 = (f32[4,256,128]{2,1,0:T(8,128)S(1)}, f32[4,256,128]{2,1,0:T(8,128)S(1)}, f32[4,256,128]{2,1,0:T(8,128)S(1)}) custom-call(s32[128]{0:T(128)S(1)} %compare_select_fusion.1.tab, bf16[256,512]{1,0:T(8,128)(2,1)S(1)} %convolution_convert_fusion.q, bf16[2,512,128]{2,1,0:T(8,128)(2,1)S(1)} %collective-permute-done.19.lo, ...), custom_call_target="tpu_custom_call" | custom-call | flops 1800000000 | tf_op jit(solution)/shard_map/far/pallas_call | solution.py:404
  64.4 2.1 %far.5 = (f32[4,256,128]{2,1,0:T(8,128)S(1)}, f32[4,256,128]{2,1,0:T(8,128)S(1)}, f32[4,256,128]{2,1,0:T(8,128)S(1)}) custom-call(s32[128]{0:T(128)S(1)} %compare_select_fusion.1.tab, bf16[256,512]{1,0:T(8,128)(2,1)S(1)} %convolution_convert_fusion.q, bf16[2,512,128]{2,1,0:T(8,128)(2,1)S(1)} %collective-permute-done.23.lo, ...), custom_call_target="tpu_custom_call" | custom-call | flops 1800000000 | tf_op jit(solution)/shard_map/far/pallas_call | solution.py:404
  66.5 2.2 %last.1.att = bf16[256,512]{1,0:T(8,128)(2,1)S(1)} custom-call(s32[128]{0:T(128)S(1)} %compare_select_fusion.1.tab, bf16[256,512]{1,0:T(8,128)(2,1)S(1)} %convolution_convert_fusion.q, bf16[2,512,128]{2,1,0:T(8,128)(2,1)S(1)} %collective-permute-done.20.lo, bf16[2,512,128]{2,1,0:T(8,128)(2,1)S(1)} %collective-permute-done.22.hi, ...), custom_call_target="tpu_custom_call" | custom-call | flops 2500000000 | tf_op jit(solution)/shard_map/last/pallas_call | solution.py:421
  68.7 2.0 %product.3 = bf16[4,256,512]{2,1,0:T(8,128)(2,1)S(1)} custom-call(s32[4]{0:T(128)S(1)} %get-tuple-element.153.cols, bf16[256,512]{1,0:T(8,128)(2,1)S(1)} %last.1.att, bf16[512,4096]{1,0:T(8,128)(2,1)S(1)} %copy-done.1), custom_call_target="tpu_custom_call" | custom-call | flops 2000000000 | tf_op jit(solution)/shard_map/product/pallas_call | solution.py:434
  70.8 2.0 %product.2.mine = f32[4,256,512]{2,1,0:T(8,128)S(1)} custom-call(s32[4]{0:T(128)S(1)} %get-tuple-element.110.cols, bf16[256,512]{1,0:T(8,128)(2,1)S(1)} %last.1.att, bf16[512,4096]{1,0:T(8,128)(2,1)S(1)} %copy-done.1), custom_call_target="tpu_custom_call" | custom-call | flops 2000000000 | tf_op jit(solution)/shard_map/product/pallas_call | solution.py:434
  72.8 0.7 collective-permute-done.25.recv
  73.5 0.7 collective-permute-start.26
  74.3 1.4 %collective-permute-start.27 = (bf16[128,512]{1,0:T(8,128)(2,1)S(1)}, bf16[128,512]{1,0:T(8,128)(2,1)S(1)}, u32[]{:S(2)}, u32[]{:S(2)}) collective-permute-start(bf16[128,512]{1,0:T(8,128)(2,1)S(1)} %get-tuple-element.155), channel_id=1, source_target_pairs={{0,192},{32,224},{64,0},{96,32},{128,64},{160,96},{192,128},{224,1... | collective-permute-start | bytes 393224 | tf_op jit(solution)/shard_map/ppermute | solution.py:51
  75.6 3.5 %collective-permute-done.26.a = bf16[128,512]{1,0:T(8,128)(2,1)S(1)} collective-permute-done((bf16[128,512]{1,0:T(8,128)(2,1)S(1)}, bf16[128,512]{1,0:T(8,128)(2,1)S(1)}, u32[]{:S(2)}, u32[]{:S(2)}) %collective-permute-start.26) | collective-permute-done | bytes 131104 | tf_op jit(solution)/shard_map/ppermute | solution.py:51
  79.1 1.6 %collective-permute-done.27.b = bf16[128,512]{1,0:T(8,128)(2,1)S(1)} collective-permute-done((bf16[128,512]{1,0:T(8,128)(2,1)S(1)}, bf16[128,512]{1,0:T(8,128)(2,1)S(1)}, u32[]{:S(2)}, u32[]{:S(2)}) %collective-permute-start.27) | collective-permute-done | bytes 131104 | tf_op jit(solution)/shard_map/ppermute | solution.py:51
  80.9 0.4 collective-permute-start.28
  81.2 1.7 %collective-permute-start.29 = (bf16[256,512]{1,0:T(8,128)(2,1)S(1)}, bf16[256,512]{1,0:T(8,128)(2,1)S(1)}, u32[]{:S(2)}, u32[]{:S(2)}) collective-permute-start(bf16[256,512]{1,0:T(8,128)(2,1)S(1)} %get-tuple-element.157), channel_id=1, source_target_pairs={{0,192},{32,224},{64,0},{96,32},{128,64},{160,96},{192,128},{224,1... | collective-permute-start | bytes 786440 | tf_op jit(solution)/shard_map/ppermute | solution.py:51
  83.0 5.2 %collective-permute-done.28.a = bf16[256,512]{1,0:T(8,128)(2,1)S(1)} collective-permute-done((bf16[256,512]{1,0:T(8,128)(2,1)S(1)}, bf16[256,512]{1,0:T(8,128)(2,1)S(1)}, u32[]{:S(2)}, u32[]{:S(2)}) %collective-permute-start.28) | collective-permute-done | bytes 262176 | tf_op jit(solution)/shard_map/ppermute | solution.py:51
  88.1 1.5 %collective-permute-done.29.b = bf16[256,512]{1,0:T(8,128)(2,1)S(1)} collective-permute-done((bf16[256,512]{1,0:T(8,128)(2,1)S(1)}, bf16[256,512]{1,0:T(8,128)(2,1)S(1)}, u32[]{:S(2)}, u32[]{:S(2)}) %collective-permute-start.29) | collective-permute-done | bytes 262176 | tf_op jit(solution)/shard_map/ppermute | solution.py:51
  89.7 0.8 final.1
  (44 shorter events, 1.4 us)
Async XLA Ops:
  0.0 25.3 %copy-start = (bf16[4096,128]{1,0:T(8,128)(2,1)S(1)}, bf16[4096,128]{1,0:T(8,128)(2,1)}, u32[]{:S(2)}) copy-start(bf16[4096,128]{1,0:T(8,128)(2,1)} %param.18) | copy-start | bytes 3145732
  0.0 10.4 %copy-start.4 = (bf16[256,4096]{1,0:T(8,128)(2,1)S(1)}, bf16[256,4096]{1,0:T(8,128)(2,1)}, u32[]{:S(2)}) copy-start(bf16[256,4096]{1,0:T(8,128)(2,1)} %param.14) | copy-start | bytes 6291460
  2.7 8.2 %copy-start.6 = (f32[4096]{0:T(1024)S(1)}, f32[4096]{0:T(1024)}, u32[]{:S(2)}) copy-start(f32[4096]{0:T(1024)} %param.15) | copy-start | bytes 49156
  5.1 6.5 %collective-permute-start.9 = (bf16[2,2,64,128]{3,2,1,0:T(8,128)(2,1)}, bf16[2,2,64,128]{3,2,1,0:T(8,128)(2,1)S(1)}, u32[]{:S(2)}, u32[]{:S(2)}) collective-permute-start(bf16[2,2,64,128]{3,2,1,0:T(8,128)(2,1)} %get-tuple-element.115), channel_id=1, source_target_pairs={{0,24},{1,25},{2,26},{3,27},{4,28},{5,29},{6,30},{7,31},{8,0},{9,1... | collective-permute-start | bytes 196616 | tf_op jit(solution)/shard_map/ppermute | solution.py:39
  8.2 6.5 %collective-permute-start.7 = (bf16[2,2,64,128]{3,2,1,0:T(8,128)(2,1)}, bf16[2,2,64,128]{3,2,1,0:T(8,128)(2,1)S(1)}, u32[]{:S(2)}, u32[]{:S(2)}) collective-permute-start(bf16[2,2,64,128]{3,2,1,0:T(8,128)(2,1)} %get-tuple-element.113), channel_id=1, source_target_pairs={{0,8},{1,9},{2,10},{3,11},{4,12},{5,13},{6,14},{7,15},{8,16},{9,17... | collective-permute-start | bytes 196616 | tf_op jit(solution)/shard_map/ppermute | solution.py:39
  8.2 6.5 %collective-permute-start.8 = (bf16[2,2,64,128]{3,2,1,0:T(8,128)(2,1)}, bf16[2,2,64,128]{3,2,1,0:T(8,128)(2,1)S(1)}, u32[]{:S(2)}, u32[]{:S(2)}) collective-permute-start(bf16[2,2,64,128]{3,2,1,0:T(8,128)(2,1)} %get-tuple-element.114), channel_id=1, source_target_pairs={{0,16},{1,17},{2,18},{3,19},{4,20},{5,21},{6,22},{7,23},{8,24},{9,... | collective-permute-start | bytes 196616 | tf_op jit(solution)/shard_map/ppermute | solution.py:39
  10.9 3.8 %copy-start.3 = (bf16[2,2,64,128]{3,2,1,0:T(8,128)(2,1)S(1)}, bf16[2,2,64,128]{3,2,1,0:T(8,128)(2,1)}, u32[]{:S(2)}) copy-start(bf16[2,2,64,128]{3,2,1,0:T(8,128)(2,1)} %get-tuple-element.112.r0) | copy-start | bytes 196612
  15.6 10.4 %copy-start.5 = (bf16[4096,128]{1,0:T(8,128)(2,1)S(1)}, bf16[4096,128]{1,0:T(8,128)(2,1)}, u32[]{:S(2)}) copy-start(bf16[4096,128]{1,0:T(8,128)(2,1)} %param.17) | copy-start | bytes 3145732
  15.6 11.2 %collective-permute-start.10 = (bf16[4,2,64,128]{3,2,1,0:T(8,128)(2,1)S(1)}, bf16[4,2,64,128]{3,2,1,0:T(8,128)(2,1)S(1)}, u32[]{:S(2)}, u32[]{:S(2)}) collective-permute-start(bf16[4,2,64,128]{3,2,1,0:T(8,128)(2,1)S(1)} %get-tuple-element.117), channel_id=1, source_target_pairs={{0,2},{1,3},{2,4},{3,5},{4,6},{5,7},{6,0},{7,1},{8,10},{9,11},{10,... | collective-permute-start | bytes 393224 | tf_op jit(solution)/shard_map/ppermute | solution.py:45
  18.9 11.1 %collective-permute-start.11 = (bf16[4,2,64,128]{3,2,1,0:T(8,128)(2,1)S(1)}, bf16[4,2,64,128]{3,2,1,0:T(8,128)(2,1)S(1)}, u32[]{:S(2)}, u32[]{:S(2)}) collective-permute-start(bf16[4,2,64,128]{3,2,1,0:T(8,128)(2,1)S(1)} %get-tuple-element.117), channel_id=1, source_target_pairs={{0,6},{1,7},{2,0},{3,1},{4,2},{5,3},{6,4},{7,5},{8,14},{9,15},{10,... | collective-permute-start | bytes 393224 | tf_op jit(solution)/shard_map/ppermute | solution.py:45
  22.0 8.1 %collective-permute-start.12 = (bf16[4,2,64,128]{3,2,1,0:T(8,128)(2,1)S(1)}, bf16[4,2,64,128]{3,2,1,0:T(8,128)(2,1)S(1)}, u32[]{:S(2)}, u32[]{:S(2)}) collective-permute-start(bf16[4,2,64,128]{3,2,1,0:T(8,128)(2,1)S(1)} %get-tuple-element.117), channel_id=1, source_target_pairs={{0,1},{1,2},{2,3},{3,4},{4,5},{5,6},{6,7},{7,0},{8,9},{9,10},{10,1... | collective-permute-start | bytes 393224 | tf_op jit(solution)/shard_map/ppermute | solution.py:45
  23.0 7.5 %collective-permute-start.13 = (bf16[4,2,64,128]{3,2,1,0:T(8,128)(2,1)S(1)}, bf16[4,2,64,128]{3,2,1,0:T(8,128)(2,1)S(1)}, u32[]{:S(2)}, u32[]{:S(2)}) collective-permute-start(bf16[4,2,64,128]{3,2,1,0:T(8,128)(2,1)S(1)} %get-tuple-element.117), channel_id=1, source_target_pairs={{0,7},{1,0},{2,1},{3,2},{4,3},{5,4},{6,5},{7,6},{8,15},{9,8},{10,9... | collective-permute-start | bytes 393224 | tf_op jit(solution)/shard_map/ppermute | solution.py:45
  25.3 3.5 %copy-start.7 = (bf16[4096,512]{1,0:T(8,128)(2,1)S(1)}, bf16[4096,512]{1,0:T(8,128)(2,1)}, u32[]{:S(2)}) copy-start(bf16[4096,512]{1,0:T(8,128)(2,1)} %param.16) | copy-start | bytes 12582916
  26.7 7.7 %collective-permute-start.16 = (bf16[256,128]{1,0:T(8,128)(2,1)S(1)}, bf16[256,128]{1,0:T(8,128)(2,1)S(1)}, u32[]{:S(2)}, u32[]{:S(2)}) collective-permute-start(bf16[256,128]{1,0:T(8,128)(2,1)S(1)} %convolution_convert_fusion.2.k), channel_id=1, source_target_pairs={{0,1},{1,2},{2,3},{3,4},{4,5},{5,6},{6,7},{7,8},{8,9},{9,10},{10,1... | collective-permute-start | bytes 196616 | tf_op jit(solution)/shard_map/ppermute | solution.py:361
  26.8 8.3 %collective-permute-start.17 = (bf16[256,128]{1,0:T(8,128)(2,1)S(1)}, bf16[256,128]{1,0:T(8,128)(2,1)S(1)}, u32[]{:S(2)}, u32[]{:S(2)}) collective-permute-start(bf16[256,128]{1,0:T(8,128)(2,1)S(1)} %convolution_convert_fusion.1.v), channel_id=1, source_target_pairs={{0,1},{1,2},{2,3},{3,4},{4,5},{5,6},{6,7},{7,8},{8,9},{9,10},{10,1... | collective-permute-start | bytes 196616 | tf_op jit(solution)/shard_map/ppermute | solution.py:361
  35.1 5.0 %collective-permute-start.18 = (bf16[4,2,64,128]{3,2,1,0:T(8,128)(2,1)S(1)}, bf16[4,2,64,128]{3,2,1,0:T(8,128)(2,1)S(1)}, u32[]{:S(2)}, u32[]{:S(2)}) collective-permute-start(bf16[4,2,64,128]{3,2,1,0:T(8,128)(2,1)S(1)} %collective-permute-done.11), channel_id=1, source_target_pairs={{0,7},{1,0},{2,1},{3,2},{4,3},{5,4},{6,5},{7,6},{8,15},{9,8},{10,9... | collective-permute-start | bytes 393224 | tf_op jit(solution)/shard_map/ppermute | solution.py:45
  35.1 7.2 %collective-permute-start.14 = (bf16[4,2,64,128]{3,2,1,0:T(8,128)(2,1)S(1)}, bf16[4,2,64,128]{3,2,1,0:T(8,128)(2,1)S(1)}, u32[]{:S(2)}, u32[]{:S(2)}) collective-permute-start(bf16[4,2,64,128]{3,2,1,0:T(8,128)(2,1)S(1)} %collective-permute-done.10), channel_id=1, source_target_pairs={{0,1},{1,2},{2,3},{3,4},{4,5},{5,6},{6,7},{7,0},{8,9},{9,10},{10,1... | collective-permute-start | bytes 393224 | tf_op jit(solution)/shard_map/ppermute | solution.py:45
  37.1 8.0 %collective-permute-start.15 = (bf16[4,2,64,128]{3,2,1,0:T(8,128)(2,1)S(1)}, bf16[4,2,64,128]{3,2,1,0:T(8,128)(2,1)S(1)}, u32[]{:S(2)}, u32[]{:S(2)}) collective-permute-start(bf16[4,2,64,128]{3,2,1,0:T(8,128)(2,1)S(1)} %collective-permute-done.10), channel_id=1, source_target_pairs={{0,2},{1,3},{2,4},{3,5},{4,6},{5,7},{6,0},{7,1},{8,10},{9,11},{10,... | collective-permute-start | bytes 393224 | tf_op jit(solution)/shard_map/ppermute | solution.py:45
  45.1 4.9 %copy-start.2 = (s32[1,4]{1,0:T(1,128)S(1)}, s32[1,4]{1,0:T(1,128)}, u32[]{:S(2)}) copy-start(s32[1,4]{1,0:T(1,128)} %offs.1) | copy-start | bytes 52
  46.7 11.0 %collective-permute-start.19 = (bf16[2,512,128]{2,1,0:T(8,128)(2,1)S(1)}, bf16[2,512,128]{2,1,0:T(8,128)(2,1)S(1)}, u32[]{:S(2)}, u32[]{:S(2)}) collective-permute-start(bf16[2,512,128]{2,1,0:T(8,128)(2,1)S(1)} %get-tuple-element.139.lo), channel_id=1, source_target_pairs={{0,8},{1,9},{2,10},{3,11},{4,12},{5,13},{6,14},{7,15},{8,16},{9,17... | collective-permute-start | bytes 786440 | tf_op jit(solution)/shard_map/ppermute | solution.py:39
  46.8 11.2 %collective-permute-start.21 = (bf16[2,512,128]{2,1,0:T(8,128)(2,1)S(1)}, bf16[2,512,128]{2,1,0:T(8,128)(2,1)S(1)}, u32[]{:S(2)}, u32[]{:S(2)}) collective-permute-start(bf16[2,512,128]{2,1,0:T(8,128)(2,1)S(1)} %get-tuple-element.140.hi), channel_id=1, source_target_pairs={{0,24},{1,25},{2,26},{3,27},{4,28},{5,29},{6,30},{7,31},{8,0},{9,1... | collective-permute-start | bytes 786440 | tf_op jit(solution)/shard_map/ppermute | solution.py:39
  52.2 10.0 %collective-permute-start.24 = (bf16[2,512,128]{2,1,0:T(8,128)(2,1)S(1)}, bf16[2,512,128]{2,1,0:T(8,128)(2,1)S(1)}, u32[]{:S(2)}, u32[]{:S(2)}) collective-permute-start(bf16[2,512,128]{2,1,0:T(8,128)(2,1)S(1)} %get-tuple-element.140.hi), channel_id=1, source_target_pairs={{0,8},{1,9},{2,10},{3,11},{4,12},{5,13},{6,14},{7,15},{8,16},{9,17... | collective-permute-start | bytes 786440 | tf_op jit(solution)/shard_map/ppermute | solution.py:39
  52.3 12.1 %collective-permute-start.23 = (bf16[2,512,128]{2,1,0:T(8,128)(2,1)S(1)}, bf16[2,512,128]{2,1,0:T(8,128)(2,1)S(1)}, u32[]{:S(2)}, u32[]{:S(2)}) collective-permute-start(bf16[2,512,128]{2,1,0:T(8,128)(2,1)S(1)} %get-tuple-element.139.lo), channel_id=1, source_target_pairs={{0,24},{1,25},{2,26},{3,27},{4,28},{5,29},{6,30},{7,31},{8,0},{9,1... | collective-permute-start | bytes 786440 | tf_op jit(solution)/shard_map/ppermute | solution.py:39
  57.7 8.8 %collective-permute-start.20 = (bf16[2,512,128]{2,1,0:T(8,128)(2,1)S(1)}, bf16[2,512,128]{2,1,0:T(8,128)(2,1)S(1)}, u32[]{:S(2)}, u32[]{:S(2)}) collective-permute-start(bf16[2,512,128]{2,1,0:T(8,128)(2,1)S(1)} %collective-permute-done.19.lo), channel_id=1, source_target_pairs={{0,8},{1,9},{2,10},{3,11},{4,12},{5,13},{6,14},{7,15},{8,16},{9,17... | collective-permute-start | bytes 786440 | tf_op jit(solution)/shard_map/ppermute | solution.py:39
  58.0 8.5 %collective-permute-start.22 = (bf16[2,512,128]{2,1,0:T(8,128)(2,1)S(1)}, bf16[2,512,128]{2,1,0:T(8,128)(2,1)S(1)}, u32[]{:S(2)}, u32[]{:S(2)}) collective-permute-start(bf16[2,512,128]{2,1,0:T(8,128)(2,1)S(1)} %collective-permute-done.21.hi), channel_id=1, source_target_pairs={{0,24},{1,25},{2,26},{3,27},{4,28},{5,29},{6,30},{7,31},{8,0},{9,1... | collective-permute-start | bytes 786440 | tf_op jit(solution)/shard_map/ppermute | solution.py:39
  66.5 2.2 %copy-start.1 = (bf16[512,4096]{1,0:T(8,128)(2,1)S(1)}, bf16[512,4096]{1,0:T(8,128)(2,1)}, u32[]{:S(2)}) copy-start(bf16[512,4096]{1,0:T(8,128)(2,1)} %w.3) | copy-start | bytes 12582916
  70.7 2.7 %collective-permute-start.25 = (bf16[4,256,512]{2,1,0:T(8,128)(2,1)S(1)}, bf16[4,256,512]{2,1,0:T(8,128)(2,1)S(1)}, u32[]{:S(2)}, u32[]{:S(2)}) collective-permute-start(bf16[4,256,512]{2,1,0:T(8,128)(2,1)S(1)} %product.3), channel_id=1, source_target_pairs={{0,32},{32,0},{64,96},{96,64},{128,160},{160,128},{192,224},{224,1... | collective-permute-start | bytes 3145736 | tf_op jit(solution)/shard_map/ppermute | solution.py:57
  73.5 5.6 %collective-permute-start.26 = (bf16[128,512]{1,0:T(8,128)(2,1)S(1)}, bf16[128,512]{1,0:T(8,128)(2,1)S(1)}, u32[]{:S(2)}, u32[]{:S(2)}) collective-permute-start(bf16[128,512]{1,0:T(8,128)(2,1)S(1)} %get-tuple-element.154), channel_id=1, source_target_pairs={{0,64},{32,96},{64,128},{96,160},{128,192},{160,224},{192,0},{224,... | collective-permute-start | bytes 393224 | tf_op jit(solution)/shard_map/ppermute | solution.py:51
  74.3 6.5 %collective-permute-start.27 = (bf16[128,512]{1,0:T(8,128)(2,1)S(1)}, bf16[128,512]{1,0:T(8,128)(2,1)S(1)}, u32[]{:S(2)}, u32[]{:S(2)}) collective-permute-start(bf16[128,512]{1,0:T(8,128)(2,1)S(1)} %get-tuple-element.155), channel_id=1, source_target_pairs={{0,192},{32,224},{64,0},{96,32},{128,64},{160,96},{192,128},{224,1... | collective-permute-start | bytes 393224 | tf_op jit(solution)/shard_map/ppermute | solution.py:51
  80.9 7.3 %collective-permute-start.28 = (bf16[256,512]{1,0:T(8,128)(2,1)S(1)}, bf16[256,512]{1,0:T(8,128)(2,1)S(1)}, u32[]{:S(2)}, u32[]{:S(2)}) collective-permute-start(bf16[256,512]{1,0:T(8,128)(2,1)S(1)} %get-tuple-element.156), channel_id=1, source_target_pairs={{0,64},{32,96},{64,128},{96,160},{128,192},{160,224},{192,0},{224,... | collective-permute-start | bytes 786440 | tf_op jit(solution)/shard_map/ppermute | solution.py:51
  81.2 8.5 %collective-permute-start.29 = (bf16[256,512]{1,0:T(8,128)(2,1)S(1)}, bf16[256,512]{1,0:T(8,128)(2,1)S(1)}, u32[]{:S(2)}, u32[]{:S(2)}) collective-permute-start(bf16[256,512]{1,0:T(8,128)(2,1)S(1)} %get-tuple-element.157), channel_id=1, source_target_pairs={{0,192},{32,224},{64,0},{96,32},{128,64},{160,96},{192,128},{224,1... | collective-permute-start | bytes 786440 | tf_op jit(solution)/shard_map/ppermute | solution.py:51
